TPU v7x, 512 devices: a whole 4x8x8 slice. The times are simulated.
512 devices in a mesh: dp: 32 (over x_hi, z, core), ctx: 16 (over x_lo, y).
Axes of the slice: x: 4 (x_hi: 2, x_lo: 2; x = x_hi * 2 + x_lo), y: 8, z: 8, core: 2. Of those that a mesh axis runs over, the one named last changes fastest.
Arguments:
- query_rows: bfloat16 [65536, 512], P(('dp', 'ctx')), may hold values from -6 to 6
- key_rows: bfloat16 [65536, 512], P(('dp', 'ctx')), may hold values from -6 to 6
- value_rows: bfloat16 [65536, 512], P(('dp', 'ctx')), may hold values from -24 to 24
- gate_rows: bfloat16 [65536, 512], P(('dp', 'ctx')), may hold values from -6 to 6
- out_weight: bfloat16 [512, 1024], replicated, may hold values from -0.25 to 0.25
- grad_out: bfloat16 [65536, 1024], P(('dp', 'ctx')), may hold values from -6 to 6
- positions: int32 [65536], P(('dp', 'ctx')), may hold values from 0 to 2047, as said below
- live_rows: int32 [65536], P(('dp', 'ctx')), may hold values from 0 to 1, as said below
Outputs:
- grad_query: bfloat16 [65536, 512], P(('dp', 'ctx'))
- grad_key: bfloat16 [65536, 512], P(('dp', 'ctx'))
- grad_value: bfloat16 [65536, 512], P(('dp', 'ctx'))
- grad_gate: bfloat16 [65536, 512], P(('dp', 'ctx'))
- grad_weight: float32 [512, 1024], replicated
Inputs may be any that keep to these rules, and one draw needn't show every extreme that they name: Within a pack, histories begin at multiples of 256 rows and hold whole multiples of 256 rows; positions count from 0 at a history's first row; in every draw some history fills a whole pack. `live_rows`: every history ends with 1 to 128 padding rows (0); all its other rows are 1.
All inputs are finite; a program needn't handle non-finite values.
Results may differ from a plain program's by a relative error of at most 0.0058.
Values may be sent and summed in bfloat16 or wider, within the bound.
A program may use at most 64 MiB of HBM per device.

v0:
```python
import math

import jax
import jax.numpy as jnp
from jax import lax
from jax.sharding import PartitionSpec as P

DH = 128
BLK = 128


norm_eps = 1e-06


def tile_allowed(query_ids, query_begins, query_alive, key_ids, key_alive):
    allowed = (
        (key_ids[None, :] <= query_ids[:, None])
        & (key_ids[None, :] >= query_begins[:, None])
        & query_alive[:, None]
        & key_alive[None, :]
    )
    return allowed.astype(jnp.float32)


def over_pack(block_fn, carry_start, kv_all):
    span = 2 * BLK
    block_count = kv_all[0].shape[0] // span

    def step(carry_in, block_index):
        first_row = block_index * span
        keys_part = lax.dynamic_slice_in_dim(kv_all[0], first_row, span)
        values_part = lax.dynamic_slice_in_dim(kv_all[1], first_row, span)
        return (block_fn(carry_in, (keys_part, values_part), first_row), None)

    result, unused = lax.scan(step, carry_start, jnp.arange(block_count, dtype=jnp.int32))
    return result


def on_device(
    query_rows, key_rows, value_rows, gate_rows, out_weight, grad_out, positions, live_rows
):
    rows_dev = query_rows.shape[0]
    features = query_rows.shape[1]
    head_count = features // DH
    score_scale = DH ** (-0.5)
    anchor = lax.axis_index("ctx") * rows_dev
    own_rows = anchor + jnp.arange(rows_dev, dtype=jnp.int32)
    own_begins = own_rows - positions
    own_alive = live_rows > 0
    all_begins, all_live = (
        lax.all_gather(own_begins, "ctx", axis=0, tiled=True),
        lax.all_gather(live_rows, "ctx", axis=0, tiled=True),
    )
    query_heads = query_rows.reshape(rows_dev, head_count, DH)
    key_heads = key_rows.reshape(rows_dev, head_count, DH)
    value_heads = value_rows.reshape(rows_dev, head_count, DH)
    zero_heads = jnp.zeros((rows_dev, head_count, DH), jnp.float32)

    def forward_block(summed, block_in, first_row):
        key_block, value_block = block_in
        row_count = key_block.shape[0]
        key_ids = first_row + jnp.arange(row_count, dtype=jnp.int32)
        key_alive = lax.dynamic_slice_in_dim(all_live, first_row, row_count) > 0
        allowed = tile_allowed(own_rows, own_begins, own_alive, key_ids, key_alive)
        scores = (
            jnp.einsum(
                "qhd,khd->hqk",
                query_heads,
                key_block.reshape(row_count, head_count, DH),
                preferred_element_type=jnp.float32,
            )
            * score_scale
        )
        weights = (scores * jax.nn.sigmoid(scores) * allowed[None]).astype(jnp.bfloat16)
        return summed + jnp.einsum(
            "hqk,khd->qhd",
            weights,
            value_block.reshape(row_count, head_count, DH),
            preferred_element_type=jnp.float32,
        )

    kv_all = (
        lax.all_gather(key_rows, "ctx", axis=0, tiled=True),
        lax.all_gather(value_rows, "ctx", axis=0, tiled=True),
    )
    attended = over_pack(forward_block, zero_heads, kv_all)
    attended = attended.reshape(rows_dev, features)
    centre = attended - jnp.mean(attended, axis=1, keepdims=True)
    inverse = lax.rsqrt(jnp.mean(centre * centre, axis=1, keepdims=True) + norm_eps)
    normed = centre * inverse
    gate_f = gate_rows.astype(jnp.float32)
    gated = (normed * gate_f).astype(jnp.bfloat16)
    grad_gated = lax.dot_general(
        grad_out, out_weight, (((1,), (1,)), ((), ())), preferred_element_type=jnp.float32
    )
    grad_gate = (grad_gated * normed).astype(jnp.bfloat16)
    grad_normed = grad_gated * gate_f
    grad_attended = inverse * (
        grad_normed
        - jnp.mean(grad_normed, axis=1, keepdims=True)
        - normed * jnp.mean(grad_normed * normed, axis=1, keepdims=True)
    )
    grad_attended = (grad_attended * own_alive.astype(jnp.float32)[:, None]).astype(jnp.bfloat16)
    grad_heads = grad_attended.reshape(rows_dev, head_count, DH)

    def query_block(summed, block_in, first_row):
        key_block, value_block = block_in
        row_count = key_block.shape[0]
        key_ids = first_row + jnp.arange(row_count, dtype=jnp.int32)
        key_alive = lax.dynamic_slice_in_dim(all_live, first_row, row_count) > 0
        key_split = key_block.reshape(row_count, head_count, DH)
        allowed = tile_allowed(own_rows, own_begins, own_alive, key_ids, key_alive)
        scores = (
            jnp.einsum("qhd,khd->hqk", query_heads, key_split, preferred_element_type=jnp.float32)
            * score_scale
        )
        sigmoid_s = jax.nn.sigmoid(scores)
        grad_weights = jnp.einsum(
            "qhd,khd->hqk",
            grad_heads,
            value_block.reshape(row_count, head_count, DH),
            preferred_element_type=jnp.float32,
        )
        grad_scores = (
            grad_weights * sigmoid_s * (1.0 + scores * (1.0 - sigmoid_s)) * allowed[None]
        ).astype(jnp.bfloat16)
        return summed + score_scale * jnp.einsum(
            "hqk,khd->qhd", grad_scores, key_split, preferred_element_type=jnp.float32
        )

    grad_query = over_pack(query_block, zero_heads, kv_all)
    query_block_in = lax.all_gather(query_rows, "ctx", axis=0, tiled=True)
    grad_block = lax.all_gather(grad_attended, "ctx", axis=0, tiled=True)
    row_count = query_block_in.shape[0]
    query_ids = jnp.arange(row_count, dtype=jnp.int32)
    query_alive = all_live > 0
    query_split = query_block_in.reshape(row_count, head_count, DH)
    grad_split = grad_block.reshape(row_count, head_count, DH)
    allowed = tile_allowed(query_ids, all_begins, query_alive, own_rows, own_alive)
    scores = (
        jnp.einsum("qhd,khd->hqk", query_split, key_heads, preferred_element_type=jnp.float32)
        * score_scale
    )
    sigmoid_s = jax.nn.sigmoid(scores)
    weights = (scores * sigmoid_s * allowed[None]).astype(jnp.bfloat16)
    grad_weights = jnp.einsum(
        "qhd,khd->hqk", grad_split, value_heads, preferred_element_type=jnp.float32
    )
    grad_scores = (
        grad_weights * sigmoid_s * (1.0 + scores * (1.0 - sigmoid_s)) * allowed[None]
    ).astype(jnp.bfloat16)
    key_sum = score_scale * jnp.einsum(
        "hqk,qhd->khd", grad_scores, query_split, preferred_element_type=jnp.float32
    )
    value_sum = jnp.einsum("hqk,qhd->khd", weights, grad_split, preferred_element_type=jnp.float32)
    grad_scale = 1.0 / math.sqrt(lax.axis_size("dp") * lax.axis_size("ctx") * rows_dev)
    local_term = lax.dot_general(
        gated, grad_out, (((0,), (0,)), ((), ())), preferred_element_type=jnp.float32
    )
    weight_total = lax.psum(local_term, ("dp", "ctx"))
    grad_weight = weight_total * grad_scale
    return (
        grad_query.reshape(rows_dev, features).astype(jnp.bfloat16),
        key_sum.reshape(rows_dev, features).astype(jnp.bfloat16),
        value_sum.reshape(rows_dev, features).astype(jnp.bfloat16),
        grad_gate,
        grad_weight,
    )


def solution(mesh):
    return jax.shard_map(
        on_device,
        mesh=mesh,
        in_specs=(
            P(("dp", "ctx"), None),
            P(("dp", "ctx"), None),
            P(("dp", "ctx"), None),
            P(("dp", "ctx"), None),
            P(),
            P(("dp", "ctx"), None),
            P(("dp", "ctx")),
            P(("dp", "ctx")),
        ),
        out_specs=(
            P(("dp", "ctx"), None),
            P(("dp", "ctx"), None),
            P(("dp", "ctx"), None),
            P(("dp", "ctx"), None),
            P(),
        ),
        check_vma=False,
    )
```

profile of v0, /device:TPU:1, one launch (start us, length us, event | category | flops | bytes accessed | tf_op | source)
XLA Modules:
  0.0 614.0 jit_solution(7695537253685259353)
XLA Ops:
  7.2 1.7 copy.66
  9.0 1.7 copy.67
  10.8 1.7 copy.68
  15.6 28.3 %all-gather = s32[16,1,128]{2,1,0:T(1,128)S(1)} all-gather(s32[1,1,128]{2,1,0:T(1,128)} %bitcast.141), channel_id=1, replica_groups=mesh['dp'=32,'ctx'=16] {'ctx'}, dimensions={0}, use_global_device_ids=true | all-gather | bytes 8704 | tf_op jit(solution)/shard_map/all_gather | solution.py:52
  43.8 23.3 %all-gather.1 = s32[16,1,128]{2,1,0:T(1,128)S(1)} all-gather(s32[1,1,128]{2,1,0:T(1,128)S(1)} %fusion.71), channel_id=1, replica_groups=mesh['dp'=32,'ctx'=16] {'ctx'}, dimensions={0}, use_global_device_ids=true | all-gather | bytes 8704 | tf_op jit(solution)/shard_map/all_gather | solution.py:51
  67.2 13.9 %all-gather.7.cloned.1.call-done = bf16[2048,512]{0,1:T(8,128)(2,1)} async-done(((bf16[128,512]{0,1:T(8,128)(2,1)}), bf16[2048,512]{0,1:T(8,128)(2,1)}) %all-gather.7.cloned.1.call-update) | async-done | bytes 2097168 | tf_op jit(solution)/shard_map/all_gather | solution.py:83
  81.1 76.6 %all-gather.9.cloned.1.call-done = bf16[2048,512]{0,1:T(8,128)(2,1)} async-done(((bf16[128,512]{0,1:T(8,128)(2,1)}), bf16[2048,512]{0,1:T(8,128)(2,1)}) %all-gather.9.cloned.1.call-update) | async-done | bytes 2097168 | tf_op jit(solution)/shard_map/all_gather | solution.py:84
  157.7 25.2 %while.22 = (s32[]{:T(128)}, f32[128,4,128]{0,2,1:T(8,128)S(1)}, s32[8]{0:T(128)S(1)}, bf16[2048,512]{0,1:T(8,128)(2,1)}, bf16[2048,512]{0,1:T(8,128)(2,1)}, /*i...) while((s32[]{:T(128)}, f32[128,4,128]{0,2,1:T(8,128)S(1)}, ...), condition=%wide.region_1.2_spmd.clone, body=%wide.region_0.1_spmd.clone.sunk | while | flops 68354696 | bytes 2495841 | solution.py:35
  162.1 1.1 constant_dynamic-slice_fusion.6
  183.3 1.9 fusion.38
  185.2 2.5 fusion.36
  189.7 27.7 %while.23 = (s32[]{:T(128)}, f32[128,4,128]{0,2,1:T(8,128)S(1)}, s32[8]{0:T(128)S(1)}, bf16[2048,512]{0,1:T(8,128)(2,1)}, bf16[2048,512]{0,1:T(8,128)(2,1)}, /*i...) while((s32[]{:T(128)}, f32[128,4,128]{0,2,1:T(8,128)S(1)}, ...), condition=%wide.region_7.8_spmd.clone, body=%wide.region_6.7_spmd.clone.sunk | while | flops 102498944 | bytes 3937641 | solution.py:35
  194.5 1.1 constant_dynamic-slice_fusion.7
  204.9 1.1 constant_dynamic-slice_fusion.7
  208.3 1.1 constant_dynamic-slice_fusion.7
  211.8 1.1 constant_dynamic-slice_fusion.7
  218.3 15.4 %all-gather.13.cloned.1.call-done = bf16[2048,512]{0,1:T(8,128)(2,1)} async-done(((bf16[128,512]{0,1:T(8,128)(2,1)}), bf16[2048,512]{0,1:T(8,128)(2,1)}) %all-gather.13.cloned.1.call-update) | async-done | bytes 2097168 | tf_op jit(solution)/shard_map/all_gather | solution.py:132
  233.7 4.4 fusion.40
  238.1 289.8 %all-reduce.2.cloned.1.call-done = f32[512,1024]{1,0:T(8,128)} async-done(((f32[512,1024]{1,0:T(8,128)}), f32[512,1024]{1,0:T(8,128)}) %all-reduce.2.cloned.1.call-update) | async-done | bytes 2097168 | tf_op jit(solution)/shard_map/psum | solution.py:160
  527.9 3.2 broadcast_multiply_fusion
  531.1 60.2 %all-gather.11.cloned.1.call-done = bf16[2048,512]{1,0:T(8,128)(2,1)} async-done(((bf16[128,512]{1,0:T(8,128)(2,1)}), bf16[2048,512]{1,0:T(8,128)(2,1)}) %all-gather.11.cloned.1.call-update) | async-done | bytes 2097168 | tf_op jit(solution)/shard_map/all_gather | solution.py:133
  591.4 4.0 copy.90
  595.3 5.8 fusion.31
  601.2 4.8 fusion.32
  (162 shorter events, 44.2 us)
Async XLA Ops:
  7.2 180.5 %copy-start = (bf16[512,1024]{1,0:T(8,128)(2,1)S(1)}, bf16[512,1024]{1,0:T(8,128)(2,1)}, u32[]{:S(2)}) copy-start(bf16[512,1024]{1,0:T(8,128)(2,1)} %param.16) | copy-start | bytes 3145732
  7.2 73.9 %all-gather.7.cloned.1.call-start = ((), (), s32[]{:S(2)}) async-start(), calls=%async_computation | async-start | bytes 2228224 | tf_op jit(solution)/shard_map/all_gather | solution.py:83
  9.0 148.7 %all-gather.9.cloned.1.call-start = ((), (), s32[]{:S(2)}) async-start(), calls=%async_computation.1 | async-start | bytes 2228224 | tf_op jit(solution)/shard_map/all_gather | solution.py:84
  10.7 223.0 %all-gather.13.cloned.1.call-start = ((), (), s32[]{:S(2)}) async-start(), calls=%async_computation.3 | async-start | bytes 2228224 | tf_op jit(solution)/shard_map/all_gather | solution.py:132
  12.5 515.4 %all-reduce.2.cloned.1.call-start = ((), (), s32[]{:S(2)}) async-start(), calls=%async_computation.4 | async-start | bytes 4194304 | tf_op jit(solution)/shard_map/psum | solution.py:160
  157.7 25.5 %copy-start.2 = (bf16[128,512]{1,0:T(8,128)(2,1)S(1)}, bf16[128,512]{1,0:T(8,128)(2,1)}, u32[]{:S(2)}) copy-start(bf16[128,512]{1,0:T(8,128)(2,1)} %param.15) | copy-start | bytes 393220
  157.7 25.5 %copy-start.4 = (bf16[128,1024]{1,0:T(8,128)(2,1)S(1)}, bf16[128,1024]{1,0:T(8,128)(2,1)}, u32[]{:S(2)}) copy-start(bf16[128,1024]{1,0:T(8,128)(2,1)} %param.17) | copy-start | bytes 786436
  185.1 406.2 %all-gather.11.cloned.1.call-start = ((), (), s32[]{:S(2)}) async-start(), calls=%async_computation.2 | async-start | bytes 2228224 | tf_op jit(solution)/shard_map/all_gather | solution.py:133
  189.0 0.7 copy-start.3
  189.7 44.0 %copy-start.5 = (bf16[128,512]{1,0:T(8,128)(2,1)S(1)}, bf16[128,512]{1,0:T(8,128)(2,1)}, u32[]{:S(2)}) copy-start(bf16[128,512]{1,0:T(8,128)(2,1)} %param.13) | copy-start | bytes 393220
  531.1 64.2 %copy-start.1 = (bf16[2048,512]{0,1:T(8,128)(2,1)S(1)}, bf16[2048,512]{0,1:T(8,128)(2,1)}, u32[]{:S(2)}) copy-start(bf16[2048,512]{0,1:T(8,128)(2,1)} %all-gather.13.cloned.1.call-done) | copy-start | bytes 6291460
  531.1 64.2 %copy-start.6 = (bf16[128,512]{1,0:T(8,128)(2,1)S(1)}, bf16[128,512]{1,0:T(8,128)(2,1)}, u32[]{:S(2)}) copy-start(bf16[128,512]{1,0:T(8,128)(2,1)} %param.14) | copy-start | bytes 393220
Sparse Core Ops, SparseCore 0:
  10.6 70.4 all-gather.6
  83.6 74.0 all-gather.8
  159.7 73.9 all-gather.12
  239.1 288.7 all-reduce.1
  530.6 60.7 all-gather.10
where the time goes:
time: 623 us; the launch traced here: 614 us
  waiting for transfers between devices  456 us (73%)
  blocking collectives  51.6 us (8%)
  local copies, waits for them, and re-layouts  39.7 us (6%)
  matrix products  28.9 us (5%)
  between operations  13.9 us (2%)
  other arithmetic  12.3 us (2%)
  loops' own time  11.4 us (2%)
    psum x1, waiting for transfers between devices, on_device(): weight_total = lax.psum(local_term, ('dp', 'ctx'))  290 us
    all_gather x1, waiting for transfers between devices, on_device(): lax.all_gather(value_rows, 'ctx', axis=0, tiled=True)  76.6 us
    all_gather x1, waiting for transfers between devices, on_device(): grad_block = lax.all_gather(grad_attended, 'ctx', axis=0, tiled=True)  60.2 us
    all_gather x1, blocking collectives, on_device(): lax.all_gather(live_rows, 'ctx', axis=0, tiled=True)  28.3 us
    all_gather x1, blocking collectives, on_device(): lax.all_gather(own_begins, 'ctx', axis=0, tiled=True)  23.3 us
    all_gather x1, waiting for transfers between devices, on_device(): query_block_in = lax.all_gather(query_rows, 'ctx', axis=0, tiled=True)  15.4 us
    all_gather x1, waiting for transfers between devices, on_device(): lax.all_gather(key_rows, 'ctx', axis=0, tiled=True)  13.9 us
  transfers between devices with their start and end apart: 5, of which 5 were waited for; matrix products, arithmetic and copies ran while one was open for 10% of the time, Pallas kernels for 0%

commit v1 on v0

v1 whole, which is shorter than its diff:
```python
import functools
import math

import jax
import jax.numpy as jnp
from jax import lax
from jax.experimental import pallas as pl
from jax.experimental.pallas import tpu as pltpu
from jax.sharding import PartitionSpec as P

DH = 128
BLK = 128
HEADS = 4
NY = 8
NX = 4
SPAN = 256
SLAB = 3 * BLK + 16
TILES = 9

norm_eps = 1e-06

BF = jnp.bfloat16
F32 = jnp.float32
MESH = pl.DeviceIdType.MESH


def dot_nt(a, b):
    return lax.dot_general(a, b, (((1,), (1,)), ((), ())), preferred_element_type=F32)


def dot_nn(a, b):
    return lax.dot_general(a, b, (((1,), (0,)), ((), ())), preferred_element_type=F32)


def dot_tn(a, b):
    return lax.dot_general(a, b, (((0,), (0,)), ((), ())), preferred_element_type=F32)


def kernel(
    n_z,
    grad_scale,
    q_in,
    k_in,
    v_in,
    gate_in,
    weight_in,
    gout_in,
    pos_in,
    live_in,
    dq_out,
    dk_out,
    dv_out,
    dgate_out,
    wa_out,
    snd,
    blk,
    fq,
    fk,
    wk,
    acc,
    asnd,
    arcv,
    gg,
    gated,
    gsnd,
    gblk,
    accq,
    acck,
    accv,
    osnd,
    orcv,
    gom,
    gatm,
    zs,
    zr,
    ys,
    yr,
    xr,
    wsum,
    wa,
    s1,
    r1,
    f1,
    s2,
    r2,
    s3,
    r3,
    f3,
    s4,
    r4,
    sm,
    rm,
    sz,
    rz,
    sy,
    ry,
    sx,
    rx,
    sya,
    rya,
    sza,
    rza,
    sca,
    rca,
):
    dp = lax.axis_index("dp")
    ctx = lax.axis_index("ctx")
    core = lax.rem(dp, 2)
    z = lax.rem(lax.div(dp, 2), n_z)
    xh = lax.div(dp, 2 * n_z)
    x = lax.div(ctx, NY)
    y = lax.rem(ctx, NY)
    x4 = 2 * xh + x
    base = dp - core
    mate = base + 1 - core
    pack = lax.div(y, HEADS)
    head = lax.rem(y, HEADS)
    quarter = 2 * x + core

    def remote(src, dst, ss, rs, to_dp, to_ctx):
        return pltpu.make_async_remote_copy(
            src_ref=src,
            dst_ref=dst,
            send_sem=ss,
            recv_sem=rs,
            device_id=(to_dp, to_ctx),
            device_id_type=MESH,
        )

    def send(src, dst, ss, rs, to_dp, to_ctx):
        own = (to_dp == dp) & (to_ctx == ctx)

        @pl.when(own)
        def _():
            pltpu.make_async_copy(src, dst, rs).start()

        @pl.when(jnp.logical_not(own))
        def _():
            remote(src, dst, ss, rs, to_dp, to_ctx).start()

    def sent(src, dst, ss, rs, to_dp, to_ctx):
        own = (to_dp == dp) & (to_ctx == ctx)

        @pl.when(jnp.logical_not(own))
        def _():
            remote(src, dst, ss, rs, to_dp, to_ctx).wait_send()

    def arrived(dst, rs):
        remote(dst, dst, rs, rs, mate, ctx).wait_recv()

    bar = pltpu.get_barrier_semaphore()
    group_at = 2 * ctx + core

    def greet_group(k, c):
        t = lax.rem(group_at + k, 32)
        pl.semaphore_signal(
            bar, inc=1, device_id=(base + lax.rem(t, 2), lax.div(t, 2)), device_id_type=MESH
        )
        return c

    lax.fori_loop(1, 32, greet_group, 0)

    def z_peer(k):
        zp = lax.rem(z + k, n_z)
        return zp, xh * 2 * n_z + zp * 2 + core

    def greet_z(k, c):
        zp, to_dp = z_peer(k)
        pl.semaphore_signal(bar, inc=1, device_id=(to_dp, ctx), device_id_type=MESH)
        return c

    lax.fori_loop(1, n_z, greet_z, 0)

    def x_peer(k):
        xp = lax.rem(x4 + k, NX)
        xhp = lax.div(xp, 2)
        return xp, dp + (xhp - xh) * 2 * n_z, lax.rem(xp, 2) * NY + y

    for other in range(2):
        pl.semaphore_signal(
            bar,
            inc=1,
            device_id=(dp + (1 - 2 * xh) * 2 * n_z, other * NY + y),
            device_id_type=MESH,
        )

    live_row = live_in[...].astype(F32)
    eye = lax.broadcasted_iota(jnp.int32, (BLK, BLK), 0) == lax.broadcasted_iota(
        jnp.int32, (BLK, BLK), 1
    )
    live_col = jnp.sum(jnp.where(eye, live_row, 0.0), axis=1, keepdims=True)
    lane = lax.broadcasted_iota(jnp.int32, (1, BLK), 1)
    begin = (ctx * BLK + lane - pos_in[...]).astype(F32) * (1.0 / SPAN)
    begin_rows = jnp.broadcast_to(begin, (16, BLK)).astype(BF)
    for h in range(HEADS):
        cols = slice(h * DH, (h + 1) * DH)
        for at, src in enumerate((q_in, k_in, v_in)):
            snd[h, at * BLK : (at + 1) * BLK, :] = (src[:, cols].astype(F32) * live_col).astype(BF)
        snd[h, 3 * BLK : SLAB, :] = begin_rows

    pl.semaphore_wait(bar, 31 + (n_z - 1) + 2)

    first_core = lax.rem(y, 2)

    def spread_args(src, dst, ss, rs, h):
        return (
            src.at[h],
            dst.at[ctx],
            ss.at[h],
            rs.at[ctx],
            base + first_core,
            x * NY + HEADS * core + h,
        )

    for h in range(HEADS):
        send(*spread_args(snd, blk, s1, r1, h))
    grad_out_to_mate = remote(gout_in, gom, sm.at[0], rm.at[0], mate, ctx)
    grad_out_to_mate.start()

    odd = lax.rem(y + core, 2)
    near = ((0, 1), (2, 7), (6, 3), (4, 5))

    def direct_block(k):
        off = jnp.where(odd == 0, near[k][0], near[k][1])
        return lax.rem(y + off, NY)

    def relay(buf, rs, fs):
        copies = []
        for k in range(4):
            b = x * NY + direct_block(k)
            arrived(buf.at[b], rs.at[b])
            copies.append(remote(buf.at[b], buf.at[b], fs.at[k], rs.at[b], dp, (1 - x) * NY + y))
            copies[-1].start()
            copies.append(remote(buf.at[b], buf.at[b], fs.at[4 + k], rs.at[b], mate, ctx))
            copies[-1].start()
        for k in range(4):
            b = (1 - x) * NY + direct_block(k)
            arrived(buf.at[b], rs.at[b])
            copies.append(remote(buf.at[b], buf.at[b], fs.at[8 + k], rs.at[b], mate, ctx))
            copies[-1].start()
        return copies

    def rest(buf, rs):
        for k in range(4):
            other = lax.rem(direct_block(k) + 1, NY)
            arrived(buf.at[x * NY + other], rs.at[x * NY + other])
        for k in range(4):
            other = lax.rem(direct_block(k) + 1, NY)
            arrived(buf.at[(1 - x) * NY + other], rs.at[(1 - x) * NY + other])

    gg[...] = dot_nt(gout_in[...], weight_in[...])

    relays1 = relay(blk, r1, f1)
    rest(blk, r1)

    half_scale = 0.5 * DH ** (-0.5)
    diff = lax.broadcasted_iota(jnp.int32, (SPAN, SPAN), 1) - lax.broadcasted_iota(
        jnp.int32, (SPAN, SPAN), 0
    )

    def part_of(at, kind):
        return blk[pl.ds(2 * at, 2), kind * BLK : (kind + 1) * BLK, :].reshape(SPAN, DH)

    def grads_of(at):
        return gblk[pl.ds(2 * at, 2), :, :].reshape(SPAN, DH)

    def reach(i_at, j_at):
        first = blk[2 * i_at, 3 * BLK : SLAB, :].astype(F32)[0:1, :]
        limit = jnp.where(first <= j_at.astype(F32), (i_at - j_at) * SPAN, -4 * SPAN)
        return jnp.concatenate([limit, limit], axis=1)

    def row_tile(t):
        first = t <= quarter
        i_at = jnp.where(first, quarter, 7 - quarter)
        j_at = jnp.where(first, t, t - quarter - 1)
        return i_at, j_at, jnp.where(first, 0, 1)

    def col_tile(t):
        first = t <= quarter
        j_at = jnp.where(first, 7 - quarter, quarter)
        i_at = jnp.where(first, 7 - quarter + t, t - 1)
        return i_at, j_at, jnp.where(first, 1, 0)

    acc[...] = jnp.zeros_like(acc)

    def forward_tile(t, c):
        i_at, j_at, slot = row_tile(t)
        u = dot_nt(part_of(i_at, 0), part_of(j_at, 1)) * half_scale
        w = jnp.where(diff <= reach(i_at, j_at), u + u * jnp.tanh(u), 0.0).astype(BF)
        acc[slot] += dot_nn(w, part_of(j_at, 2))
        return c

    lax.fori_loop(0, TILES, forward_tile, 0)

    asnd[...] = acc[...].reshape(2, 2, BLK, DH).astype(BF)

    def back_args(src, dst, ss, rs, slot, half):
        i_at = quarter if slot == 0 else 7 - quarter
        return (
            src.at[slot, half],
            dst.at[head],
            ss.at[2 * slot + half],
            rs.at[head],
            base + pack,
            2 * i_at + half,
        )

    for slot in range(2):
        for half in range(2):
            send(*back_args(asnd, arcv, s2, r2, slot, half))

    def slopes(u):
        t = jnp.tanh(u)
        return t, 0.5 * ((1.0 + t) + u * (1.0 - t * t))

    def row_slopes(t, c):
        i_at, j_at, slot = row_tile(t)
        u = dot_nt(part_of(i_at, 0), part_of(j_at, 1)) * half_scale
        _, f = slopes(u)
        fq[t] = jnp.where(diff <= reach(i_at, j_at), f, 0.0)
        return c

    def col_slopes(t, c):
        i_at, j_at, slot = col_tile(t)
        u = dot_nt(part_of(j_at, 1), part_of(i_at, 0)) * half_scale
        th, f = slopes(u)
        seen = -diff <= reach(i_at, j_at)
        fk[t] = jnp.where(seen, f, 0.0)
        wk[t] = jnp.where(seen, u + u * th, 0.0).astype(BF)
        return c

    for h in range(HEADS):
        arrived(arcv.at[h], r2.at[h])

    att = [arcv[h].astype(F32) for h in range(HEADS)]

    def row_mean(parts):
        total = parts[0] + parts[1] + parts[2] + parts[3]
        return jnp.sum(total, axis=1, keepdims=True) * (1.0 / (HEADS * DH))

    mean = row_mean(att)
    centre = [a - mean for a in att]
    inverse = lax.rsqrt(row_mean([a * a for a in centre]) + norm_eps)
    normed = [a * inverse for a in centre]
    gate = [gate_in[:, h * DH : (h + 1) * DH].astype(F32) for h in range(HEADS)]
    grad_gated = [gg[:, h * DH : (h + 1) * DH] for h in range(HEADS)]
    grad_normed = [a * b for a, b in zip(grad_gated, gate)]
    mean_1 = row_mean(grad_normed)
    mean_2 = row_mean([a * b for a, b in zip(grad_normed, normed)])
    factor = inverse * live_col
    for h in range(HEADS):
        gsnd[h] = (factor * (grad_normed[h] - mean_1 - normed[h] * mean_2)).astype(BF)
        send(*spread_args(gsnd, gblk, s3, r3, h))
    for h in range(HEADS):
        gated[h // 2, :, (h % 2) * DH : (h % 2 + 1) * DH] = (normed[h] * gate[h]).astype(BF)
    gated_to_mate = remote(gated.at[1 - core], gatm, sm.at[1], rm.at[1], mate, ctx)
    gated_to_mate.start()
    for h in range(HEADS):
        dgate_out[:, h * DH : (h + 1) * DH] = (grad_gated[h] * normed[h]).astype(BF)

    arrived(gom, rm.at[0])
    arrived(gatm, rm.at[1])
    part = dot_tn(gated[core], gout_in[...]) + dot_tn(gatm[...], gom[...])
    rows_z = 2 * BLK // n_z
    zs[...] = part.reshape(n_z, rows_z, part.shape[1]).astype(BF)

    def z_args(k):
        zp, to_dp = z_peer(k)
        return zs.at[zp], zr.at[z], sz.at[k - 1], rz.at[z], to_dp, ctx

    def z_send(k, c):
        remote(*z_args(k)).start()
        return c

    lax.fori_loop(1, n_z, z_send, 0)

    lax.fori_loop(0, TILES, row_slopes, 0)
    lax.fori_loop(0, TILES, col_slopes, 0)

    relays3 = relay(gblk, r3, f3)
    rest(gblk, r3)

    accq[...] = jnp.zeros_like(accq)
    acck[...] = jnp.zeros_like(acck)
    accv[...] = jnp.zeros_like(accv)

    def query_tile(t, c):
        i_at, j_at, slot = row_tile(t)
        ds = (dot_nt(grads_of(i_at), part_of(j_at, 2)) * fq[t]).astype(BF)
        accq[slot] += dot_nn(ds, part_of(j_at, 1))
        return c

    def key_tile(t, c):
        i_at, j_at, slot = col_tile(t)
        grads = grads_of(i_at)
        ds = (dot_nt(part_of(j_at, 2), grads) * fk[t]).astype(BF)
        acck[slot] += dot_nn(ds, part_of(i_at, 0))
        accv[slot] += dot_nn(wk[t], grads)
        return c

    lax.fori_loop(0, TILES, query_tile, 0)
    lax.fori_loop(0, TILES, key_tile, 0)

    score_scale = DH ** (-0.5)
    for slot in range(2):
        for half in range(2):
            rows = slice(half * BLK, (half + 1) * BLK)
            osnd[slot, half, 0] = (accq[slot, rows, :] * score_scale).astype(BF)
            osnd[slot, half, 1] = (acck[slot, rows, :] * score_scale).astype(BF)
            osnd[slot, half, 2] = accv[slot, rows, :].astype(BF)
            send(*back_args(osnd, orcv, s4, r4, slot, half))

    total = zs[z].astype(F32)

    def z_sum(k, total):
        zp, _ = z_peer(k)
        arrived(zr.at[zp], rz.at[zp])
        return total + zr[zp].astype(F32)

    total = lax.fori_loop(1, n_z, z_sum, total)
    for at in range(NY):
        ys[at] = total[:, at * BLK : (at + 1) * BLK]

    def y_peer(k):
        yp = lax.rem(y + k, NY)
        return yp, x * NY + yp

    def y_args(k):
        yp, to_ctx = y_peer(k)
        return ys.at[yp], yr.at[y], sy.at[k - 1], ry.at[y], dp, to_ctx

    def y_send(k, c):
        remote(*y_args(k)).start()
        return c

    lax.fori_loop(1, NY, y_send, 0)

    def y_sum(k, total):
        yp, _ = y_peer(k)
        arrived(yr.at[yp], ry.at[yp])
        return total + yr[yp]

    wsum[...] = lax.fori_loop(1, NY, y_sum, ys[y])

    def x_args(k):
        xp, to_dp, to_ctx = x_peer(k)
        return wsum, xr.at[x4], sx.at[k - 1], rx.at[x4], to_dp, to_ctx

    for k in range(1, NX):
        remote(*x_args(k)).start()
    xr[x4] = wsum[...]
    for k in range(1, NX):
        xp, _, _ = x_peer(k)
        arrived(xr.at[xp], rx.at[xp])
    summed = (xr[0] + xr[1]) + (xr[2] + xr[3])
    wa[core, z, y] = (summed * grad_scale).astype(BF)

    def ya_args(k):
        yp, to_ctx = y_peer(k)
        own = wa.at[core, z, y]
        return own, own, sya.at[k - 1], rya.at[y], dp, to_ctx

    def ya_send(k, c):
        remote(*ya_args(k)).start()
        return c

    lax.fori_loop(1, NY, ya_send, 0)

    def ya_wait(k, c):
        yp, _ = y_peer(k)
        arrived(wa.at[core, z, yp], rya.at[yp])
        return c

    lax.fori_loop(1, NY, ya_wait, 0)

    def za_args(k):
        zp, to_dp = z_peer(k)
        own = wa.at[core, z]
        return own, own, sza.at[k - 1], rza.at[z], to_dp, ctx

    def za_send(k, c):
        remote(*za_args(k)).start()
        return c

    lax.fori_loop(1, n_z, za_send, 0)

    def ca_args(at):
        own = wa.at[core, at]
        return own, own, sca.at[at], rca.at[at], mate, ctx

    remote(*ca_args(z)).start()

    for h in range(HEADS):
        arrived(orcv.at[h], r4.at[h])
        cols = slice(h * DH, (h + 1) * DH)
        dq_out[:, cols] = orcv[h, 0]
        dk_out[:, cols] = orcv[h, 1]
        dv_out[:, cols] = orcv[h, 2]

    def za_wait(k, c):
        zp, _ = z_peer(k)
        arrived(wa.at[core, zp], rza.at[zp])
        remote(*ca_args(zp)).start()
        return c

    lax.fori_loop(1, n_z, za_wait, 0)

    def ca_wait(at, c):
        arrived(wa.at[1 - core, at], rca.at[at])
        remote(*ca_args(at)).wait_send()
        return c

    lax.fori_loop(0, n_z, ca_wait, 0)

    wa_out[...] = wa[...]

    for h in range(HEADS):
        sent(*spread_args(snd, blk, s1, r1, h))
        sent(*spread_args(gsnd, gblk, s3, r3, h))
    for slot in range(2):
        for half in range(2):
            sent(*back_args(asnd, arcv, s2, r2, slot, half))
            sent(*back_args(osnd, orcv, s4, r4, slot, half))
    for copy in relays1 + relays3 + [grad_out_to_mate, gated_to_mate]:
        copy.wait_send()

    def z_done(k, c):
        remote(*z_args(k)).wait_send()
        remote(*za_args(k)).wait_send()
        return c

    lax.fori_loop(1, n_z, z_done, 0)

    def y_done(k, c):
        remote(*y_args(k)).wait_send()
        remote(*ya_args(k)).wait_send()
        return c

    lax.fori_loop(1, NY, y_done, 0)
    for k in range(1, NX):
        remote(*x_args(k)).wait_send()


def on_device(
    n_z, query_rows, key_rows, value_rows, gate_rows, out_weight, grad_out, positions, live_rows
):
    rows, features = query_rows.shape
    width = grad_out.shape[1]
    grad_scale = 1.0 / math.sqrt(lax.axis_size("dp") * lax.axis_size("ctx") * rows)
    rows_z = 2 * BLK // n_z
    vmem = pl.BlockSpec(memory_space=pltpu.VMEM)
    dma = pltpu.SemaphoreType.DMA
    out_rows = jax.ShapeDtypeStruct((rows, features), BF)
    dq, dk, dv, dgate, wa = pl.pallas_call(
        functools.partial(kernel, n_z, grad_scale),
        out_shape=[out_rows] * 4 + [jax.ShapeDtypeStruct((2, n_z, NY, rows_z, BLK), BF)],
        in_specs=[vmem] * 8,
        out_specs=[vmem] * 5,
        scratch_shapes=[
            pltpu.VMEM((HEADS, SLAB, DH), BF),
            pltpu.VMEM((16, SLAB, DH), BF),
            pltpu.VMEM((TILES, SPAN, SPAN), F32),
            pltpu.VMEM((TILES, SPAN, SPAN), F32),
            pltpu.VMEM((TILES, SPAN, SPAN), BF),
            pltpu.VMEM((2, SPAN, DH), F32),
            pltpu.VMEM((2, 2, BLK, DH), BF),
            pltpu.VMEM((HEADS, BLK, DH), BF),
            pltpu.VMEM((rows, features), F32),
            pltpu.VMEM((2, rows, features // 2), BF),
            pltpu.VMEM((HEADS, BLK, DH), BF),
            pltpu.VMEM((16, BLK, DH), BF),
            pltpu.VMEM((2, SPAN, DH), F32),
            pltpu.VMEM((2, SPAN, DH), F32),
            pltpu.VMEM((2, SPAN, DH), F32),
            pltpu.VMEM((2, 2, 3, BLK, DH), BF),
            pltpu.VMEM((HEADS, 3, BLK, DH), BF),
            pltpu.VMEM((rows, width), BF),
            pltpu.VMEM((rows, features // 2), BF),
            pltpu.VMEM((n_z, rows_z, width), BF),
            pltpu.VMEM((n_z, rows_z, width), BF),
            pltpu.VMEM((NY, rows_z, BLK), F32),
            pltpu.VMEM((NY, rows_z, BLK), F32),
            pltpu.VMEM((NX, rows_z, BLK), F32),
            pltpu.VMEM((rows_z, BLK), F32),
            pltpu.VMEM((2, n_z, NY, rows_z, BLK), BF),
            dma((HEADS,)),
            dma((16,)),
            dma((12,)),
            dma((4,)),
            dma((HEADS,)),
            dma((HEADS,)),
            dma((16,)),
            dma((12,)),
            dma((4,)),
            dma((HEADS,)),
            dma((2,)),
            dma((2,)),
            dma((n_z,)),
            dma((n_z,)),
            dma((NY,)),
            dma((NY,)),
            dma((NX,)),
            dma((NX,)),
            dma((NY,)),
            dma((NY,)),
            dma((n_z,)),
            dma((n_z,)),
            dma((n_z,)),
            dma((n_z,)),
        ],
        compiler_params=pltpu.CompilerParams(
            collective_id=0, has_side_effects=True, vmem_limit_bytes=40 * 1024 * 1024
        ),
    )(
        query_rows,
        key_rows,
        value_rows,
        gate_rows,
        out_weight,
        grad_out,
        positions.reshape(1, rows),
        live_rows.reshape(1, rows),
    )
    grad_weight = jnp.transpose(wa, (0, 1, 3, 2, 4)).reshape(features, width).astype(F32)
    return dq, dk, dv, dgate, grad_weight


def solution(mesh):
    n_z = mesh.shape["dp"] // 4
    return jax.shard_map(
        functools.partial(on_device, n_z),
        mesh=mesh,
        in_specs=(
            P(("dp", "ctx"), None),
            P(("dp", "ctx"), None),
            P(("dp", "ctx"), None),
            P(("dp", "ctx"), None),
            P(),
            P(("dp", "ctx"), None),
            P(("dp", "ctx")),
            P(("dp", "ctx")),
        ),
        out_specs=(
            P(("dp", "ctx"), None),
            P(("dp", "ctx"), None),
            P(("dp", "ctx"), None),
            P(("dp", "ctx"), None),
            P(),
        ),
        check_vma=False,
    )
```

time: 623 us -> 117 us (0.19); the launches traced: 614 us -> 116 us
  waiting for transfers between devices: 456 us -> 0 us
  Pallas kernels: 0 us -> 102 us
  blocking collectives: 51.6 us -> 0 us
  matrix products: 28.9 us -> 0 us
  local copies, waits for them, and re-layouts: 39.7 us -> 13.1 us
  between operations: 13.9 us -> 0.67 us
  other arithmetic: 12.3 us -> 0.28 us
  loops' own time: 11.4 us -> 0 us
    psum x1 -> x0, waiting for transfers between devices: 290 us -> none  [on_device(): weight_total = lax.psum(local_term, ('dp', 'ctx'))]
    all_gather x4 -> x0, waiting for transfers between devices: 166 us -> none  [the longest x1 76.6 us: on_device(): lax.all_gather(value_rows, 'ctx', axis=0, tiled=True)]
    pallas_call x0 -> x1, Pallas kernels: none -> 102 us  [on_device(): pl.pallas_call(functools.partial(kernel, n_z, grad_scale), out_shape=[out...]
    all_gather x2 -> x0, blocking collectives: 51.6 us -> none  [the longest x1 28.3 us: on_device(): lax.all_gather(live_rows, 'ctx', axis=0, tiled=True)]
    dot_general x29 -> x0, matrix products: 28.9 us -> none  [the longest x1 5.82 us: on_device(): jnp.einsum('hqk,qhd->khd', grad_scores, query_split, preferred_element_ty...]
    dynamic_slice x32 -> x0, local copies, waits for them, and re-layouts: 26.6 us -> none  [the longest x16 9.38 us: over_pack(): lax.scan(step, carry_start, jnp.arange(block_count, dtype=jnp.int32))]
    another operation x2 -> x0, loops' own time: 11.4 us -> none  [over_pack(): lax.scan(step, carry_start, jnp.arange(block_count, dtype=jnp.int32))]
  transfers between devices with their start and end apart: 5 -> 0, of which waited for: 5 -> 0; matrix products, arithmetic and copies ran while one was open for 10% -> 0% of each run, Pallas kernels for 0% -> 0%
where the time goes in v1:
time: 117 us; the launch traced here: 116 us
  Pallas kernels  102 us (87%)
  local copies, waits for them, and re-layouts  13.1 us (11%)
    pallas_call x1, Pallas kernels, on_device(): pl.pallas_call(functools.partial(kernel, n_z, grad_scale), out_shape=[out...  102 us
    unnamed x21, local copies, waits for them, and re-layouts  11.5 us

profile of v1, /device:TPU:1, one launch (start us, length us, event | category | flops | bytes accessed | tf_op | source)
XLA Modules:
  0.0 116.3 jit_solution(4895798630844530148)
XLA Ops:
  0.6 0.0 copy-start
  0.6 1.2 %copy-done = bf16[512,1024]{1,0:T(8,128)(2,1)S(1)} copy-done((bf16[512,1024]{1,0:T(8,128)(2,1)S(1)}, bf16[512,1024]{1,0:T(8,128)(2,1)}, u32[]{:S(2)}) %copy-start) | copy-done | bytes 1048600
  1.9 0.0 copy-start.1
  1.9 0.9 copy-done.1
  2.8 0.0 copy-start.2
  2.8 0.9 copy-done.2
  3.7 0.0 copy-start.3
  3.7 0.9 copy-done.3
  4.6 0.0 copy-start.4
  4.6 0.9 copy-done.4
  5.5 0.0 copy-start.5
  5.5 0.9 copy-done.5
  6.4 0.0 copy-start.6
  6.4 0.7 copy-done.6
  7.1 0.0 copy-start.7
  7.1 0.7 copy-done.7
  7.7 102.2 %shard_map.119 = (bf16[128,512]{1,0:T(8,128)(2,1)S(1)}, bf16[128,512]{1,0:T(8,128)(2,1)S(1)}, bf16[128,512]{1,0:T(8,128)(2,1)S(1)}, bf16[128,512]{1,0:T(8,128)(2,1)S(1)}, bf16[2,8,8,32,128]{4,3,2,1,0:T(8,128)(2,1)S(1)}) custom-call(bf16[128,512]{1,0:T(8,128)(2,1)S(1)} %copy-done.2, bf16[128,512]{1,0:T(8,128)(2,1)S(1)} %copy-done.3, ...), custom_call_target="tpu_custom_call" | custom-call | tf_op jit(solution)/shard_map/pallas_call | solution.py:554
  109.9 0.3 convert_bitcast_fusion
  110.2 1.6 %copy.13 = f32[2,8,32,8,128]{4,3,2,1,0:T(8,128)S(1)} copy(f32[2,8,32,8,128]{4,2,3,1,0:T(8,128)S(1)} %convert_bitcast_fusion) | data formatting | bytes 4194304 | tf_op jit(solution)/shard_map/convert_element_type | solution.py:624
  111.9 1.8 %copy.16 = f32[64,8,8,128]{3,1,2,0:T(8,128)} copy(f32[64,8,8,128]{3,2,1,0:T(8,128)S(1)} %bitcast.11) | data formatting | bytes 4194304
  113.6 0.7 copy.21
  114.3 0.7 copy.22
  115.0 0.7 copy.23
  115.6 0.7 copy.24
Async XLA Ops:
  0.6 1.2 %copy-start = (bf16[512,1024]{1,0:T(8,128)(2,1)S(1)}, bf16[512,1024]{1,0:T(8,128)(2,1)}, u32[]{:S(2)}) copy-start(bf16[512,1024]{1,0:T(8,128)(2,1)} %weight_in.1) | copy-start | bytes 3145732
  1.9 0.9 copy-start.1
  2.8 0.9 copy-start.2
  3.7 0.9 copy-start.3
  4.6 0.9 copy-start.4
  5.5 0.9 copy-start.5
  6.4 0.7 copy-start.6
  7.1 0.7 copy-start.7

commit v2 on v0

v2 whole, which is shorter than its diff:
```python
import functools
import math

import jax
import jax.numpy as jnp
from jax import lax
from jax.experimental import pallas as pl
from jax.experimental.pallas import tpu as pltpu
from jax.sharding import PartitionSpec as P

DH = 128
BLK = 128
HEADS = 4
NY = 8
NZ = 8
NX = 4
SPAN = 256
SLAB = 3 * BLK + 16
TILES = 9
VLIM = 60
FEAT = 64
HALF = 512

norm_eps = 1e-06

BF = jnp.bfloat16
F32 = jnp.float32
MESH = pl.DeviceIdType.MESH


def dot_nt(a, b):
    return lax.dot_general(a, b, (((1,), (1,)), ((), ())), preferred_element_type=F32)


def dot_nn(a, b):
    return lax.dot_general(a, b, (((1,), (0,)), ((), ())), preferred_element_type=F32)


def scratch():
    vmem = pltpu.VMEM
    dma = pltpu.SemaphoreType.DMA
    return dict(
        q=vmem((BLK, HEADS * DH), BF),
        k=vmem((BLK, HEADS * DH), BF),
        v=vmem((BLK, HEADS * DH), BF),
        gate=vmem((BLK, HEADS * DH), BF),
        weight=vmem((HEADS * DH, 2 * HALF), BF),
        gout=vmem((BLK, 2 * HALF), BF),
        pos=vmem((1, BLK), jnp.int32),
        live=vmem((1, BLK), jnp.int32),
        snd=vmem((HEADS, SLAB, DH), BF),
        blk=vmem((16, SLAB, DH), BF),
        asnd=vmem((HEADS, 2, BLK, DH), BF),
        aux=vmem((2, 2, 2, BLK, DH), BF),
        gg=vmem((BLK, HEADS * DH), F32),
        dgate=vmem((BLK, HEADS * DH), BF),
        gz=vmem((NZ, 2, BLK, HALF), BF),
        fq=vmem((TILES, SPAN, SPAN), F32),
        fk=vmem((TILES, SPAN, SPAN), F32),
        wk=vmem((TILES, SPAN, SPAN), BF),
        acc=vmem((2, SPAN, DH), F32),
        stats=vmem((HEADS, 2, 8, SPAN), F32),
        gtsnd=vmem((2, 2, DH, BLK), BF),
        gt=vmem((2 * NZ, FEAT, BLK), BF),
        nsnd=vmem((2, 2, BLK, DH), BF),
        nrcv=vmem((HEADS, BLK, DH), BF),
        gblk=vmem((16, BLK, DH), BF),
        accq=vmem((2, SPAN, DH), F32),
        acck=vmem((2, SPAN, DH), F32),
        accv=vmem((2, SPAN, DH), F32),
        osnd=vmem((2, 2, 3, BLK, DH), BF),
        orcv=vmem((HEADS, 3, BLK, DH), BF),
        ysnd=vmem((NY, FEAT // 2, BLK), BF),
        yrcv=vmem((NY, FEAT // 2, BLK), BF),
        xrcv=vmem((NX, FEAT // 2, BLK), F32),
        wsum=vmem((FEAT // 2, BLK), F32),
        wa=vmem((2, NZ, NY, FEAT // 4, BLK), BF),
        wb=vmem((2, NY, NZ, FEAT // 4, BLK), BF),
        load=dma((8,)),
        write=dma((17,)),
        s1=dma((HEADS,)),
        r1=dma((16,)),
        f1=dma((12,)),
        sa=dma((HEADS,)),
        ra=dma((4,)),
        sm=dma((1,)),
        rm=dma((1,)),
        szp=dma((NZ,)),
        szm=dma((NZ,)),
        rgz=dma((NZ,)),
        sst=dma((HEADS,)),
        rst=dma((HEADS,)),
        sgt=dma((8,)),
        rgt=dma((2 * NZ,)),
        fgt=dma((NZ,)),
        sg=dma((6,)),
        rg=dma((8,)),
        sn=dma((4,)),
        rn=dma((HEADS,)),
        s4=dma((4,)),
        r4=dma((HEADS,)),
        sy=dma((NY,)),
        ry=dma((NY,)),
        sx=dma((NX,)),
        rx=dma((NX,)),
        sa1=dma((NY,)),
        ra1=dma((NY,)),
        sa2=dma((NZ,)),
        ra2=dma((NZ,)),
        sb1=dma((NZ,)),
        rb1=dma((NZ,)),
        sb2=dma((NY,)),
        rb2=dma((NY,)),
        sca=dma((NZ,)),
        rca=dma((NZ,)),
        scb=dma((NY,)),
        rcb=dma((NY,)),
    )


def kernel(grad_scale, *refs):
    q_in, k_in, v_in, gate_in, weight_in, gout_in, pos_in, live_in = refs[:8]
    dq_out, dk_out, dv_out, dgate_out, wa_out, wb_out = refs[8:14]
    (
        q,
        k,
        v,
        gate,
        weight,
        gout,
        pos,
        live,
        snd,
        blk,
        asnd,
        aux,
        gg,
        dgate,
        gz,
        fq,
        fk,
        wk,
        acc,
        stats,
        gtsnd,
        gt,
        nsnd,
        nrcv,
        gblk,
        accq,
        acck,
        accv,
        osnd,
        orcv,
        ysnd,
        yrcv,
        xrcv,
        wsum,
        wa,
        wb,
        load,
        write,
        s1,
        r1,
        f1,
        sa,
        ra,
        sm,
        rm,
        szp,
        szm,
        rgz,
        sst,
        rst,
        sgt,
        rgt,
        fgt,
        sg,
        rg,
        sn,
        rn,
        s4,
        r4,
        sy,
        ry,
        sx,
        rx,
        sa1,
        ra1,
        sa2,
        ra2,
        sb1,
        rb1,
        sb2,
        rb2,
        sca,
        rca,
        scb,
        rcb,
    ) = refs[14:]
    dp = lax.axis_index("dp")
    ctx = lax.axis_index("ctx")
    core = lax.rem(dp, 2)
    z = lax.rem(lax.div(dp, 2), NZ)
    xh = lax.div(dp, 2 * NZ)
    x = lax.div(ctx, NY)
    y = lax.rem(ctx, NY)
    x4 = 2 * xh + x
    base = dp - core
    mate = base + 1 - core
    pack = lax.div(y, HEADS)
    head = lax.rem(y, HEADS)
    quarter = 2 * x + core
    over_x = (1 - x) * NY + y

    drains = []
    stores = iter(range(17))

    def store(src, dst):
        copy = pltpu.make_async_copy(src, dst, write.at[next(stores)])
        copy.start()
        drains.append(copy.wait)

    def remote(src, dst, ss, rs, to_dp, to_ctx):
        return pltpu.make_async_remote_copy(
            src_ref=src,
            dst_ref=dst,
            send_sem=ss,
            recv_sem=rs,
            device_id=(to_dp, to_ctx),
            device_id_type=MESH,
        )

    def push(*args):
        copy = remote(*args)
        copy.start()
        drains.append(copy.wait_send)

    def send(src, dst, ss, rs, to_dp, to_ctx):
        own = (to_dp == dp) & (to_ctx == ctx)
        copy = remote(src, dst, ss, rs, to_dp, to_ctx)

        @pl.when(own)
        def _():
            pltpu.make_async_copy(src, dst, rs).start()

        @pl.when(jnp.logical_not(own))
        def _():
            copy.start()

        def drain():
            @pl.when(jnp.logical_not(own))
            def _():
                copy.wait_send()

        drains.append(drain)

    def each(count, first, body):
        def step(k, c):
            body(k)
            return c

        lax.fori_loop(first, count, step, 0)

    def tiles(body):
        for t in range(TILES):
            body(t)

    def push_each(count, args):
        each(count, 1, lambda k: remote(*args(k)).start())
        drains.append(lambda: each(count, 1, lambda k: remote(*args(k)).wait_send()))

    def arrived(dst, rs):
        remote(dst, dst, rs, rs, mate, ctx).wait_recv()

    def x_peer(k):
        xp = lax.rem(x4 + k, NX)
        return xp, dp + (lax.div(xp, 2) - xh) * 2 * NZ, lax.rem(xp, 2) * NY + y

    def y_peer(k):
        yp = lax.rem(y + k, NY)
        return yp, x * NY + yp

    def z_peer(k):
        zp = lax.rem(z + k, NZ)
        return zp, dp + (zp - z) * 2

    def place_of(block):
        i_at = lax.div(block, 2)
        low = i_at < 4
        return jnp.where(low, i_at, 7 - i_at), jnp.where(low, 0, 1), lax.rem(block, 2)

    loads = [
        pltpu.make_async_copy(src, dst, load.at[at])
        for at, (src, dst) in enumerate(
            (
                (live_in, live),
                (pos_in, pos),
                (q_in, q),
                (k_in, k),
                (v_in, v),
                (gout_in, gout),
                (weight_in, weight),
                (gate_in, gate),
            )
        )
    ]
    for copy in loads:
        copy.start()

    bar = pltpu.get_barrier_semaphore()

    def greet(to_dp, to_ctx):
        pl.semaphore_signal(bar, inc=1, device_id=(to_dp, to_ctx), device_id_type=MESH)

    group_at = 2 * ctx + core

    def greet_group(k):
        t = lax.rem(group_at + k, 32)
        greet(base + lax.rem(t, 2), lax.div(t, 2))

    each(32, 1, greet_group)
    each(NZ, 1, lambda k: greet(z_peer(k)[1], ctx))
    for other in range(2):
        greet(dp + (1 - 2 * xh) * 2 * NZ, other * NY + y)
    own_quarter, own_slot, own_half = place_of(ctx)
    handler_core = lax.rem(own_quarter, 2)
    handler_x = lax.div(own_quarter, 2)

    def greet_gated(k):
        zp = lax.rem(z + k, NZ)
        greet(
            (xh * NZ + zp) * 2 + handler_core, handler_x * NY + core * HEADS + lax.div(z, 2)
        )

    each(NZ, 1, greet_gated)
    away = jnp.where(lax.div(z, 2) == head, 4, 8)

    for copy in loads[:5]:
        copy.wait()
    live_row = live[...].astype(F32)
    eye = lax.broadcasted_iota(jnp.int32, (BLK, BLK), 0) == lax.broadcasted_iota(
        jnp.int32, (BLK, BLK), 1
    )
    live_col = jnp.sum(jnp.where(eye, live_row, 0.0), axis=1, keepdims=True)
    lane = lax.broadcasted_iota(jnp.int32, (1, BLK), 1)
    begin = (ctx * BLK + lane - pos[...]).astype(F32) * (1.0 / SPAN)
    begin_rows = jnp.broadcast_to(begin, (16, BLK)).astype(BF)
    for h in range(HEADS):
        cols = slice(h * DH, (h + 1) * DH)
        for at, src in enumerate((q, k, v)):
            snd[h, at * BLK : (at + 1) * BLK, :] = (src[:, cols].astype(F32) * live_col).astype(BF)
        snd[h, 3 * BLK : SLAB, :] = begin_rows

    pl.semaphore_wait(bar, 31 + (NZ - 1) + 2 + away)

    first_core = lax.rem(y, 2)
    for h in range(HEADS):
        to_ctx = x * NY + HEADS * core + h
        send(snd.at[h], blk.at[ctx], s1.at[h], r1.at[ctx], base + first_core, to_ctx)

    loads[5].wait()
    gz[z, core] = gout[:, pl.ds(pl.multiple_of(core * HALF, HALF), HALF)]
    push(
        gout.at[:, pl.ds(pl.multiple_of((1 - core) * HALF, HALF), HALF)],
        gz.at[z, core],
        sm.at[0],
        rm.at[0],
        mate,
        ctx,
    )

    arrived(gz.at[z, 1 - core], rm.at[0])
    z_up, z_down = z_peer(1)[1], z_peer(NZ - 1)[1]

    def ring_up(at):
        push(gz.at[at], gz.at[at], szp.at[at], rgz.at[at], z_up, ctx)

    def ring_down(at):
        push(gz.at[at], gz.at[at], szm.at[at], rgz.at[at], z_down, ctx)

    def ring_take(k):
        at = z_peer(k)[0]
        arrived(gz.at[at], rgz.at[at])
        return at

    ring_up(z)
    ring_down(z)

    loads[6].wait()
    loads[7].wait()
    gg[...] = dot_nt(gout[...], weight[...])
    grad_normed = gg[...] * gate[...].astype(F32)
    mean_1 = jnp.sum(grad_normed, axis=1, keepdims=True) * (1.0 / (HEADS * DH))
    grad_centred = ((grad_normed - mean_1) * live_col).astype(BF)
    for h in range(HEADS):
        cols = slice(h * DH, (h + 1) * DH)
        asnd[h, 0] = grad_centred[:, cols]
        asnd[h, 1] = gate[:, cols]

    odd = lax.rem(y + core, 2)
    near = ((0, 1), (2, 7), (6, 3), (4, 5))

    def direct_y(at):
        return lax.rem(y + jnp.where(odd == 0, near[at][0], near[at][1]), NY)

    def hand_direct(at):
        b = x * NY + direct_y(at)
        arrived(blk.at[b], r1.at[b])
        push(blk.at[b], blk.at[b], f1.at[at], r1.at[b], dp, over_x)
        push(blk.at[b], blk.at[b], f1.at[4 + at], r1.at[b], mate, ctx)

    def hand_crossed(at):
        b = (1 - x) * NY + direct_y(at)
        arrived(blk.at[b], r1.at[b])
        push(blk.at[b], blk.at[b], f1.at[8 + at], r1.at[b], mate, ctx)

    hand_direct(0)
    hand_direct(1)
    ring_up(ring_take(NZ - 1))
    ring_down(ring_take(1))
    hand_direct(2)
    hand_direct(3)
    for h in range(HEADS):
        send(
            asnd.at[h],
            aux.at[own_slot, own_half],
            sa.at[h],
            ra.at[2 * own_slot + own_half],
            base + handler_core,
            handler_x * NY + core * HEADS + h,
        )
    for at in range(4):
        hand_crossed(at)
    ring_up(ring_take(NZ - 2))
    ring_down(ring_take(2))
    for at in range(8):
        row = x if at < 4 else 1 - x
        b = row * NY + lax.rem(direct_y(at % 4) + 1, NY)
        arrived(blk.at[b], r1.at[b])

    half_scale = 0.5 * DH ** (-0.5)
    diff = lax.broadcasted_iota(jnp.int32, (SPAN, SPAN), 1) - lax.broadcasted_iota(
        jnp.int32, (SPAN, SPAN), 0
    )

    def part_of(at, kind):
        return blk[pl.ds(2 * at, 2), kind * BLK : (kind + 1) * BLK, :].reshape(SPAN, DH)

    def grads_of(at):
        return gblk[pl.ds(2 * at, 2), :, :].reshape(SPAN, DH)

    def reach(i_at, j_at):
        first = blk[2 * i_at, 3 * BLK : SLAB, :].astype(F32)[0:1, :]
        limit = jnp.where(first <= j_at.astype(F32), (i_at - j_at) * SPAN, -4 * SPAN)
        return jnp.concatenate([limit, limit], axis=1)

    def row_tile(t):
        first = t <= quarter
        i_at = jnp.where(first, quarter, 7 - quarter)
        j_at = jnp.where(first, t, t - quarter - 1)
        return i_at, j_at, jnp.where(first, 0, 1)

    def col_tile(t):
        first = t <= quarter
        j_at = jnp.where(first, 7 - quarter, quarter)
        i_at = jnp.where(first, 7 - quarter + t, t - 1)
        return i_at, j_at, jnp.where(first, 1, 0)

    acc[...] = jnp.zeros_like(acc)

    def forward_tile(t):
        i_at, j_at, slot = row_tile(t)
        u = dot_nt(part_of(i_at, 0), part_of(j_at, 1)) * half_scale
        w = jnp.where(diff <= reach(i_at, j_at), u + u * jnp.tanh(u), 0.0).astype(BF)
        acc[slot] += dot_nn(w, part_of(j_at, 2))

    tiles(forward_tile)

    for at in range(4):
        arrived(aux.at[at // 2, at % 2], ra.at[at])
    column = lax.broadcasted_iota(jnp.int32, (SPAN, DH), 1)
    for slot in range(2):
        att = acc[slot]
        grads = aux[slot, :, 0].reshape(SPAN, DH).astype(F32)
        mean_h = jnp.sum(att, axis=1, keepdims=True) * (1.0 / DH)
        centre = att - mean_h
        square = jnp.sum(centre * centre, axis=1, keepdims=True)
        grad_sum = jnp.sum(grads, axis=1, keepdims=True)
        cross = jnp.sum(grads * centre, axis=1, keepdims=True)
        table = jnp.where(
            column == 0,
            mean_h,
            jnp.where(column == 1, square, jnp.where(column == 2, grad_sum, cross)),
        )
        stats[head, slot] = jnp.transpose(table)[0:8, :]

    def stats_args(at):
        other = lax.rem(head + at, HEADS)
        mine = stats.at[head]
        return mine, mine, sst.at[at], rst.at[head], dp, x * NY + HEADS * pack + other

    for at in range(1, HEADS):
        push(*stats_args(at))

    def slopes(u):
        th = jnp.tanh(u)
        return th, 0.5 * ((1.0 + th) + u * (1.0 - th * th))

    def row_slopes(t):
        i_at, j_at, slot = row_tile(t)
        u = dot_nt(part_of(i_at, 0), part_of(j_at, 1)) * half_scale
        _, f = slopes(u)
        fq[t] = jnp.where(diff <= reach(i_at, j_at), f, 0.0)

    def col_slopes(t):
        i_at, j_at, slot = col_tile(t)
        u = dot_nt(part_of(j_at, 1), part_of(i_at, 0)) * half_scale
        th, f = slopes(u)
        seen = -diff <= reach(i_at, j_at)
        fk[t] = jnp.where(seen, f, 0.0)
        wk[t] = jnp.where(seen, u + u * th, 0.0).astype(BF)

    tiles(row_slopes)
    ring_up(ring_take(NZ - 3))

    for at in range(1, HEADS):
        other = lax.rem(head + at, HEADS)
        arrived(stats.at[other], rst.at[other])
    line = lax.broadcasted_iota(jnp.int32, (DH, SPAN), 0)
    grads_by_slot = []
    for slot in range(2):
        of = [[stats[h, slot, at : at + 1, :] for at in range(4)] for h in range(HEADS)]
        mean = (of[0][0] + of[1][0] + of[2][0] + of[3][0]) * (1.0 / HEADS)
        square = 0.0
        cross = 0.0
        for mean_h, square_h, grad_h, cross_h in of:
            away_h = mean_h - mean
            square = square + (square_h + DH * away_h * away_h)
            cross = cross + (cross_h + away_h * grad_h)
        inverse = lax.rsqrt(square * (1.0 / (HEADS * DH)) + norm_eps)
        mean_2 = inverse * cross * (1.0 / (HEADS * DH))
        table = jnp.transpose(
            jnp.where(line == 0, mean, jnp.where(line == 1, inverse, mean_2))
        )
        inverse = table[:, 1:2]
        normed = (acc[slot] - table[:, 0:1]) * inverse
        gated = normed * aux[slot, :, 1].reshape(SPAN, DH).astype(F32)
        gated_t = jnp.transpose(gated).astype(BF)
        i_at = quarter if slot == 0 else 7 - quarter
        for half in range(2):
            gtsnd[slot, half] = gated_t[:, half * BLK : (half + 1) * BLK]
            for part in range(2):
                to_z = 2 * head + part
                send(
                    gtsnd.at[slot, half, pl.ds(part * FEAT, FEAT)],
                    gt.at[2 * z + pack],
                    sgt.at[4 * slot + 2 * half + part],
                    rgt.at[2 * z + pack],
                    (xh * NZ + to_z) * 2 + pack,
                    2 * i_at + half,
                )
        grads = inverse * (
            aux[slot, :, 0].reshape(SPAN, DH).astype(F32) - normed * table[:, 2:3]
        )
        gblk[pl.ds(2 * i_at, 2)] = grads.astype(BF).reshape(2, BLK, DH)
        mine = gblk.at[pl.ds(2 * i_at, 2)]
        push(mine, mine, sg.at[3 * slot], rg.at[i_at], dp, over_x)
        push(mine, mine, sg.at[3 * slot + 1], rg.at[i_at], mate, over_x)
        push(mine, mine, sg.at[3 * slot + 2], rg.at[i_at], mate, ctx)
        nsnd[slot] = normed.astype(BF).reshape(2, BLK, DH)

    def back(src, dst, ss, rs, slot, half):
        i_at = quarter if slot == 0 else 7 - quarter
        send(
            src.at[slot, half],
            dst.at[head],
            ss.at[2 * slot + half],
            rs.at[head],
            base + pack,
            2 * i_at + half,
        )

    for slot in range(2):
        for half in range(2):
            back(nsnd, nrcv, sn, rn, slot, half)

    tiles(col_slopes)

    for at in range(1, 4):
        other = lax.rem(quarter + at, 4)
        for i_at in (other, 7 - other):
            arrived(gblk.at[pl.ds(2 * i_at, 2)], rg.at[i_at])

    accq[...] = jnp.zeros_like(accq)
    acck[...] = jnp.zeros_like(acck)
    accv[...] = jnp.zeros_like(accv)

    def query_tile(t):
        i_at, j_at, slot = row_tile(t)
        ds = (dot_nt(grads_of(i_at), part_of(j_at, 2)) * fq[t]).astype(BF)
        accq[slot] += dot_nn(ds, part_of(j_at, 1))

    def key_tile(t):
        i_at, j_at, slot = col_tile(t)
        grads = grads_of(i_at)
        ds = (dot_nt(part_of(j_at, 2), grads) * fk[t]).astype(BF)
        acck[slot] += dot_nn(ds, part_of(i_at, 0))
        accv[slot] += dot_nn(wk[t], grads)

    tiles(query_tile)
    tiles(key_tile)

    def gated_forward(zp):
        at = 2 * zp + core
        return gt.at[at], gt.at[at], fgt.at[zp], rgt.at[at], mate, ctx

    def gated_take(zp):
        arrived(gt.at[2 * zp + core], rgt.at[2 * zp + core])
        remote(*gated_forward(zp)).start()

    each(NZ, 0, gated_take)
    drains.append(lambda: each(NZ, 0, lambda zp: remote(*gated_forward(zp)).wait_send()))
    ring_take(NZ - 4)
    ring_take(3)
    each(NZ, 0, lambda zp: arrived(gt.at[2 * zp + 1 - core], rgt.at[2 * zp + 1 - core]))
    total = jnp.zeros((FEAT, HALF), F32)
    for zp in range(NZ):
        features = jnp.concatenate([gt[2 * zp], gt[2 * zp + 1]], axis=1)
        total = total + dot_nn(features, gz[zp].reshape(2 * BLK, HALF))
    for at in range(NY):
        rows, cols = at // 4 * (FEAT // 2), at % 4 * BLK
        ysnd[at] = total[rows : rows + FEAT // 2, cols : cols + BLK].astype(BF)

    def y_args(k):
        yp, to_ctx = y_peer(k)
        return ysnd.at[yp], yrcv.at[y], sy.at[k], ry.at[y], dp, to_ctx

    push_each(NY, y_args)

    score_scale = DH ** (-0.5)
    for slot in range(2):
        for half in range(2):
            rows = slice(half * BLK, (half + 1) * BLK)
            osnd[slot, half, 0] = (accq[slot, rows, :] * score_scale).astype(BF)
            osnd[slot, half, 1] = (acck[slot, rows, :] * score_scale).astype(BF)
            osnd[slot, half, 2] = accv[slot, rows, :].astype(BF)
            back(osnd, orcv, s4, r4, slot, half)

    def y_sum(k, total):
        yp = y_peer(k)[0]
        arrived(yrcv.at[yp], ry.at[yp])
        return total + yrcv[yp].astype(F32)

    wsum[...] = lax.fori_loop(1, NY, y_sum, ysnd[y].astype(F32))

    def x_args(k):
        _, to_dp, to_ctx = x_peer(k)
        return wsum, xrcv.at[x4], sx.at[k], rx.at[x4], to_dp, to_ctx

    for k_x in range(1, NX):
        push(*x_args(k_x))
    xrcv[x4] = wsum[...]

    for h in range(HEADS):
        cols = slice(h * DH, (h + 1) * DH)
        arrived(nrcv.at[h], rn.at[h])
        dgate[:, cols] = (gg[:, cols] * nrcv[h].astype(F32)).astype(BF)
    store(dgate, dgate_out)

    for k_x in range(1, NX):
        xp = x_peer(k_x)[0]
        arrived(xrcv.at[xp], rx.at[xp])
    summed = ((xrcv[0] + xrcv[1]) + (xrcv[2] + xrcv[3])) * grad_scale
    wa[core, z, y] = summed[0 : FEAT // 4].astype(BF)
    wb[core, y, z] = summed[FEAT // 4 : FEAT // 2].astype(BF)

    def a1_args(k):
        mine = wa.at[core, z, y]
        return mine, mine, sa1.at[k], ra1.at[y], dp, y_peer(k)[1]

    def b1_args(k):
        mine = wb.at[core, y, z]
        return mine, mine, sb1.at[k], rb1.at[z], z_peer(k)[1], ctx

    def a2_args(k):
        mine = wa.at[core, z]
        return mine, mine, sa2.at[k], ra2.at[z], z_peer(k)[1], ctx

    def b2_args(k):
        mine = wb.at[core, y]
        return mine, mine, sb2.at[k], rb2.at[y], dp, y_peer(k)[1]

    def ca_args(zp):
        mine = wa.at[core, zp]
        return mine, mine, sca.at[zp], rca.at[zp], mate, ctx

    def cb_args(yp):
        mine = wb.at[core, yp]
        return mine, mine, scb.at[yp], rcb.at[yp], mate, ctx

    push_each(NY, a1_args)
    push_each(NZ, b1_args)

    def a1_take(k):
        yp = y_peer(k)[0]
        arrived(wa.at[core, z, yp], ra1.at[yp])

    def b1_take(k):
        zp = z_peer(k)[0]
        arrived(wb.at[core, y, zp], rb1.at[zp])

    each(NY, 1, a1_take)
    push_each(NZ, a2_args)
    each(NZ, 1, b1_take)
    push_each(NY, b2_args)
    remote(*ca_args(z)).start()
    remote(*cb_args(y)).start()

    for h in range(HEADS):
        cols = slice(h * DH, (h + 1) * DH)
        arrived(orcv.at[h], r4.at[h])
        for at, out in enumerate((dq_out, dk_out, dv_out)):
            store(orcv.at[h, at], out.at[:, cols])

    def last_take(k):
        zp = z_peer(k)[0]
        arrived(wa.at[core, zp], ra2.at[zp])
        remote(*ca_args(zp)).start()
        yp = y_peer(k)[0]
        arrived(wb.at[core, yp], rb2.at[yp])
        remote(*cb_args(yp)).start()

    each(NY, 1, last_take)
    store(wa.at[core], wa_out.at[core])
    store(wb.at[core], wb_out.at[core])

    def from_mate(at):
        arrived(wa.at[1 - core, at], rca.at[at])
        arrived(wb.at[1 - core, at], rcb.at[at])
        remote(*ca_args(at)).wait_send()
        remote(*cb_args(at)).wait_send()

    each(NZ, 0, from_mate)

    store(wa.at[1 - core], wa_out.at[1 - core])
    store(wb.at[1 - core], wb_out.at[1 - core])

    for drain in drains:
        drain()


def writer(*refs):
    ins, outs, held, sems = refs[:6], refs[6:11], refs[11:18], refs[18]
    loads = [
        pltpu.make_async_copy(src, dst, sems.at[at])
        for at, (src, dst) in enumerate(zip(ins, held[:6], strict=True))
    ]
    for copy in loads[4:] + loads[:4]:
        copy.start()
    wa, wb, gw = held[4:]
    for copy in loads[4:]:
        copy.wait()
    copies = []
    for zp in range(NZ):
        for c in range(2):
            for at in range(NY):
                first = zp * FEAT + at // 4 * (FEAT // 2)
                cols = slice(c * HALF + at % 4 * BLK, c * HALF + at % 4 * BLK + BLK)
                gw[first : first + 16, cols] = wa[c, zp, at].astype(F32)
                gw[first + 16 : first + 32, cols] = wb[c, at, zp].astype(F32)
        rows = pl.ds(zp * FEAT, FEAT)
        copies.append(pltpu.make_async_copy(gw.at[rows], outs[4].at[rows], sems.at[6 + zp]))
        copies[-1].start()
    for at in range(4):
        loads[at].wait()
        copies.append(pltpu.make_async_copy(held[at], outs[at], sems.at[14 + at]))
        copies[-1].start()
    for copy in copies:
        copy.wait()


def on_device(
    query_rows, key_rows, value_rows, gate_rows, out_weight, grad_out, positions, live_rows
):
    rows, features = query_rows.shape
    width = grad_out.shape[1]
    grad_scale = 1.0 / math.sqrt(lax.axis_size("dp") * lax.axis_size("ctx") * rows)
    held = scratch()
    out_rows = jax.ShapeDtypeStruct((rows, features), BF)
    slabs = jax.ShapeDtypeStruct((2, 8, 8, FEAT // 4, BLK), BF)
    anywhere = pl.BlockSpec(memory_space=pl.ANY)
    parts = pl.pallas_call(
        functools.partial(kernel, grad_scale),
        out_shape=[out_rows] * 4 + [slabs] * 2,
        in_specs=[anywhere] * 8,
        out_specs=[anywhere] * 6,
        scratch_shapes=list(held.values()),
        compiler_params=pltpu.CompilerParams(
            collective_id=0, has_side_effects=True, vmem_limit_bytes=VLIM * 1024 * 1024
        ),
    )(
        query_rows,
        key_rows,
        value_rows,
        gate_rows,
        out_weight,
        grad_out,
        positions.reshape(1, rows),
        live_rows.reshape(1, rows),
    )
    return pl.pallas_call(
        writer,
        out_shape=[out_rows] * 4 + [jax.ShapeDtypeStruct((features, width), F32)],
        in_specs=[anywhere] * 6,
        out_specs=[anywhere] * 5,
        scratch_shapes=[
            *[pltpu.VMEM(out_rows.shape, BF)] * 4,
            *[pltpu.VMEM(slabs.shape, BF)] * 2,
            pltpu.VMEM((features, width), F32),
            pltpu.SemaphoreType.DMA((18,)),
        ],
        compiler_params=pltpu.CompilerParams(vmem_limit_bytes=VLIM * 1024 * 1024),
    )(*parts)


def solution(mesh):
    rows = P(("dp", "ctx"), None)
    return jax.shard_map(
        on_device,
        mesh=mesh,
        in_specs=(rows, rows, rows, rows, P(), rows, P(("dp", "ctx")), P(("dp", "ctx"))),
        out_specs=(rows, rows, rows, rows, P()),
        check_vma=False,
    )
```

time: 623 us -> 94.8 us (0.15); the launches traced: 614 us -> 94.7 us
  waiting for transfers between devices: 456 us -> 0 us
  Pallas kernels: 0 us -> 94 us
  blocking collectives: 51.6 us -> 0 us
  local copies, waits for them, and re-layouts: 39.7 us -> 0 us
  matrix products: 28.9 us -> 0 us
  between operations: 13.9 us -> 0.64 us
  other arithmetic: 12.3 us -> 0 us
  loops' own time: 11.4 us -> 0 us
    psum x1 -> x0, waiting for transfers between devices: 290 us -> none  [on_device(): weight_total = lax.psum(local_term, ('dp', 'ctx'))]
    all_gather x4 -> x0, waiting for transfers between devices: 166 us -> none  [the longest x1 76.6 us: on_device(): lax.all_gather(value_rows, 'ctx', axis=0, tiled=True)]
    pallas_call x0 -> x2, Pallas kernels: none -> 94 us  [the longest x1 91.2 us: on_device(): pl.pallas_call(functools.partial(kernel, grad_scale), out_shape=[out_rows...]
    all_gather x2 -> x0, blocking collectives: 51.6 us -> none  [the longest x1 28.3 us: on_device(): lax.all_gather(live_rows, 'ctx', axis=0, tiled=True)]
    dot_general x29 -> x0, matrix products: 28.9 us -> none  [the longest x1 5.82 us: on_device(): jnp.einsum('hqk,qhd->khd', grad_scores, query_split, preferred_element_ty...]
    dynamic_slice x32 -> x0, local copies, waits for them, and re-layouts: 26.6 us -> none  [the longest x16 9.38 us: over_pack(): lax.scan(step, carry_start, jnp.arange(block_count, dtype=jnp.int32))]
    another operation x2 -> x0, loops' own time: 11.4 us -> none  [over_pack(): lax.scan(step, carry_start, jnp.arange(block_count, dtype=jnp.int32))]
    unnamed x21 -> x0, local copies, waits for them, and re-layouts: 8.31 us -> none
  transfers between devices with their start and end apart: 5 -> 0, of which waited for: 5 -> 0; matrix products, arithmetic and copies ran while one was open for 10% -> 0% of each run, Pallas kernels for 0% -> 0%
where the time goes in v2:
time: 94.8 us; the launch traced here: 94.7 us
  Pallas kernels  94 us (99%)
    pallas_call x1, Pallas kernels, on_device(): pl.pallas_call(functools.partial(kernel, grad_scale), out_shape=[out_rows...  91.2 us
    pallas_call x1, Pallas kernels, on_device(): pl.pallas_call(writer, out_shape=[out_rows] * 4 + [jax.ShapeDtypeStruct((...  2.85 us

profile of v2, /device:TPU:1, one launch (start us, length us, event | category | flops | bytes accessed | tf_op | source)
XLA Modules:
  0.0 94.7 jit_solution(15825829073866719233)
XLA Ops:
  0.6 91.2 %shard_map.119 = (bf16[128,512]{1,0:T(8,128)(2,1)}, bf16[128,512]{1,0:T(8,128)(2,1)}, bf16[128,512]{1,0:T(8,128)(2,1)}, bf16[128,512]{1,0:T(8,128)(2,1)}, bf16[2...) custom-call(bf16[128,512]{1,0:T(8,128)(2,1)} %refs_0_.1, bf16[128,512]{1,0:T(8,128)(2,1)} %refs_1_.1, ...), custom_call_target="tpu_custom_call" | custom-call | tf_op jit(solution)/shard_map/pallas_call | solution.py:793
  91.8 2.8 %shard_map.120 = (bf16[128,512]{1,0:T(8,128)(2,1)}, bf16[128,512]{1,0:T(8,128)(2,1)}, bf16[128,512]{1,0:T(8,128)(2,1)}, bf16[128,512]{1,0:T(8,128)(2,1)}, f32[512,1024]{1,0:T(8,128)}) custom-call(bf16[128,512]{1,0:T(8,128)(2,1)} %get-tuple-element.11.refs_0_, bf16[128,512]{1,0:T(8,128)(2,1)} %get-tuple-element.12.refs_1_, ...), custom_call_target="tpu_custom_call" | custom-call | tf_op jit(solution)/shard_map/pallas_call | solution.py:812

commit v3 on v2

--- a/solution.py
+++ b/solution.py
@@ -566,8 +566,7 @@
         gblk[pl.ds(2 * i_at, 2)] = grads.astype(BF).reshape(2, BLK, DH)
         mine = gblk.at[pl.ds(2 * i_at, 2)]
         push(mine, mine, sg.at[3 * slot], rg.at[i_at], dp, over_x)
-        push(mine, mine, sg.at[3 * slot + 1], rg.at[i_at], mate, over_x)
-        push(mine, mine, sg.at[3 * slot + 2], rg.at[i_at], mate, ctx)
+        push(mine, mine, sg.at[3 * slot + 1], rg.at[i_at], mate, ctx)
         nsnd[slot] = normed.astype(BF).reshape(2, BLK, DH)
 
     def back(src, dst, ss, rs, slot, half):
@@ -581,35 +580,13 @@
             2 * i_at + half,
         )
 
-    for slot in range(2):
-        for half in range(2):
-            back(nsnd, nrcv, sn, rn, slot, half)
-
     tiles(col_slopes)
 
-    for at in range(1, 4):
-        other = lax.rem(quarter + at, 4)
-        for i_at in (other, 7 - other):
-            arrived(gblk.at[pl.ds(2 * i_at, 2)], rg.at[i_at])
-
-    accq[...] = jnp.zeros_like(accq)
-    acck[...] = jnp.zeros_like(acck)
-    accv[...] = jnp.zeros_like(accv)
-
-    def query_tile(t):
-        i_at, j_at, slot = row_tile(t)
-        ds = (dot_nt(grads_of(i_at), part_of(j_at, 2)) * fq[t]).astype(BF)
-        accq[slot] += dot_nn(ds, part_of(j_at, 1))
-
-    def key_tile(t):
-        i_at, j_at, slot = col_tile(t)
-        grads = grads_of(i_at)
-        ds = (dot_nt(part_of(j_at, 2), grads) * fk[t]).astype(BF)
-        acck[slot] += dot_nn(ds, part_of(i_at, 0))
-        accv[slot] += dot_nn(wk[t], grads)
-
-    tiles(query_tile)
-    tiles(key_tile)
+    crossed = lax.rem(quarter + 2, 4)
+    for at, i_at in enumerate((crossed, 7 - crossed)):
+        theirs = gblk.at[pl.ds(2 * i_at, 2)]
+        arrived(theirs, rg.at[i_at])
+        push(theirs, theirs, sg.at[3 * at + 2], rg.at[i_at], mate, ctx)
 
     def gated_forward(zp):
         at = 2 * zp + core
@@ -638,6 +615,34 @@
 
     push_each(NY, y_args)
 
+    for slot in range(2):
+        for half in range(2):
+            back(nsnd, nrcv, sn, rn, slot, half)
+
+    for at in (1, 3):
+        other = lax.rem(quarter + at, 4)
+        for i_at in (other, 7 - other):
+            arrived(gblk.at[pl.ds(2 * i_at, 2)], rg.at[i_at])
+
+    accq[...] = jnp.zeros_like(accq)
+    acck[...] = jnp.zeros_like(acck)
+    accv[...] = jnp.zeros_like(accv)
+
+    def query_tile(t):
+        i_at, j_at, slot = row_tile(t)
+        ds = (dot_nt(grads_of(i_at), part_of(j_at, 2)) * fq[t]).astype(BF)
+        accq[slot] += dot_nn(ds, part_of(j_at, 1))
+
+    def key_tile(t):
+        i_at, j_at, slot = col_tile(t)
+        grads = grads_of(i_at)
+        ds = (dot_nt(part_of(j_at, 2), grads) * fk[t]).astype(BF)
+        acck[slot] += dot_nn(ds, part_of(i_at, 0))
+        accv[slot] += dot_nn(wk[t], grads)
+
+    tiles(query_tile)
+    tiles(key_tile)
+
     score_scale = DH ** (-0.5)
     for slot in range(2):
         for half in range(2):
@@ -645,7 +650,6 @@
             osnd[slot, half, 0] = (accq[slot, rows, :] * score_scale).astype(BF)
             osnd[slot, half, 1] = (acck[slot, rows, :] * score_scale).astype(BF)
             osnd[slot, half, 2] = accv[slot, rows, :].astype(BF)
-            back(osnd, orcv, s4, r4, slot, half)
 
     def y_sum(k, total):
         yp = y_peer(k)[0]
@@ -701,6 +705,10 @@
 
     push_each(NY, a1_args)
     push_each(NZ, b1_args)
+
+    for slot in range(2):
+        for half in range(2):
+            back(osnd, orcv, s4, r4, slot, half)
 
     def a1_take(k):
         yp = y_peer(k)[0]

time: 94.8 us -> 91.9 us (0.969)
  Pallas kernels: 94 us -> 91.1 us
    pallas_call x1, Pallas kernels: 91.2 us -> 88.2 us  [on_device(): pl.pallas_call(functools.partial(kernel, grad_scale), out_shape=[out_rows...]
where the time goes in v3:
time: 91.9 us; the launch traced here: 91.7 us
  Pallas kernels  91.1 us (99%)
    pallas_call x1, Pallas kernels, on_device(): pl.pallas_call(functools.partial(kernel, grad_scale), out_shape=[out_rows...  88.2 us
    pallas_call x1, Pallas kernels, on_device(): pl.pallas_call(writer, out_shape=[out_rows] * 4 + [jax.ShapeDtypeStruct((...  2.85 us

profile of v3, /device:TPU:1, one launch (start us, length us, event | category | flops | bytes accessed | tf_op | source)
XLA Modules:
  0.0 91.7 jit_solution(4660703516191579794)
XLA Ops:
  0.6 88.2 %shard_map.119 = (bf16[128,512]{1,0:T(8,128)(2,1)}, bf16[128,512]{1,0:T(8,128)(2,1)}, bf16[128,512]{1,0:T(8,128)(2,1)}, bf16[128,512]{1,0:T(8,128)(2,1)}, bf16[2...) custom-call(bf16[128,512]{1,0:T(8,128)(2,1)} %refs_0_.1, bf16[128,512]{1,0:T(8,128)(2,1)} %refs_1_.1, ...), custom_call_target="tpu_custom_call" | custom-call | tf_op jit(solution)/shard_map/pallas_call | solution.py:801
  88.9 2.8 %shard_map.120 = (bf16[128,512]{1,0:T(8,128)(2,1)}, bf16[128,512]{1,0:T(8,128)(2,1)}, bf16[128,512]{1,0:T(8,128)(2,1)}, bf16[128,512]{1,0:T(8,128)(2,1)}, f32[512,1024]{1,0:T(8,128)}) custom-call(bf16[128,512]{1,0:T(8,128)(2,1)} %get-tuple-element.11.refs_0_, bf16[128,512]{1,0:T(8,128)(2,1)} %get-tuple-element.12.refs_1_, ...), custom_call_target="tpu_custom_call" | custom-call | tf_op jit(solution)/shard_map/pallas_call | solution.py:820

commit v4 on v3

--- a/solution.py
+++ b/solution.py
@@ -74,10 +74,10 @@
         yrcv=vmem((NY, FEAT // 2, BLK), BF),
         xrcv=vmem((NX, FEAT // 2, BLK), F32),
         wsum=vmem((FEAT // 2, BLK), F32),
-        wa=vmem((2, NZ, NY, FEAT // 4, BLK), BF),
-        wb=vmem((2, NY, NZ, FEAT // 4, BLK), BF),
+        wa=vmem((2, NZ, NY, FEAT // 2, BLK), BF),
         load=dma((8,)),
-        write=dma((17,)),
+        write=dma((13,)),
+        slabs=dma((2, NZ)),
         s1=dma((HEADS,)),
         r1=dma((16,)),
         f1=dma((12,)),
@@ -107,20 +107,14 @@
         ra1=dma((NY,)),
         sa2=dma((NZ,)),
         ra2=dma((NZ,)),
-        sb1=dma((NZ,)),
-        rb1=dma((NZ,)),
-        sb2=dma((NY,)),
-        rb2=dma((NY,)),
         sca=dma((NZ,)),
         rca=dma((NZ,)),
-        scb=dma((NY,)),
-        rcb=dma((NY,)),
     )
 
 
 def kernel(grad_scale, *refs):
     q_in, k_in, v_in, gate_in, weight_in, gout_in, pos_in, live_in = refs[:8]
-    dq_out, dk_out, dv_out, dgate_out, wa_out, wb_out = refs[8:14]
+    dq_out, dk_out, dv_out, dgate_out, wa_out = refs[8:13]
     (
         q,
         k,
@@ -157,9 +151,9 @@
         xrcv,
         wsum,
         wa,
-        wb,
         load,
         write,
+        slabs,
         s1,
         r1,
         f1,
@@ -189,15 +183,9 @@
         ra1,
         sa2,
         ra2,
-        sb1,
-        rb1,
-        sb2,
-        rb2,
         sca,
         rca,
-        scb,
-        rcb,
-    ) = refs[14:]
+    ) = refs[13:]
     dp = lax.axis_index("dp")
     ctx = lax.axis_index("ctx")
     core = lax.rem(dp, 2)
@@ -214,7 +202,7 @@
     over_x = (1 - x) * NY + y
 
     drains = []
-    stores = iter(range(17))
+    stores = iter(range(13))
 
     def store(src, dst):
         copy = pltpu.make_async_copy(src, dst, write.at[next(stores)])
@@ -676,54 +664,37 @@
         xp = x_peer(k_x)[0]
         arrived(xrcv.at[xp], rx.at[xp])
     summed = ((xrcv[0] + xrcv[1]) + (xrcv[2] + xrcv[3])) * grad_scale
-    wa[core, z, y] = summed[0 : FEAT // 4].astype(BF)
-    wb[core, y, z] = summed[FEAT // 4 : FEAT // 2].astype(BF)
+    wa[core, z, y] = summed.astype(BF)
 
     def a1_args(k):
         mine = wa.at[core, z, y]
         return mine, mine, sa1.at[k], ra1.at[y], dp, y_peer(k)[1]
 
-    def b1_args(k):
-        mine = wb.at[core, y, z]
-        return mine, mine, sb1.at[k], rb1.at[z], z_peer(k)[1], ctx
-
     def a2_args(k):
         mine = wa.at[core, z]
         return mine, mine, sa2.at[k], ra2.at[z], z_peer(k)[1], ctx
 
-    def b2_args(k):
-        mine = wb.at[core, y]
-        return mine, mine, sb2.at[k], rb2.at[y], dp, y_peer(k)[1]
-
     def ca_args(zp):
         mine = wa.at[core, zp]
         return mine, mine, sca.at[zp], rca.at[zp], mate, ctx
 
-    def cb_args(yp):
-        mine = wb.at[core, yp]
-        return mine, mine, scb.at[yp], rcb.at[yp], mate, ctx
+    def slab_store(c, zp):
+        return pltpu.make_async_copy(wa.at[c, zp], wa_out.at[c, zp], slabs.at[c, zp])
 
     push_each(NY, a1_args)
-    push_each(NZ, b1_args)
-
+
+    def a1_take(k):
+        yp = y_peer(k)[0]
+        arrived(wa.at[core, z, yp], ra1.at[yp])
+
+    each(NY, 1, a1_take)
+    push_each(NZ, a2_args)
     for slot in range(2):
         for half in range(2):
             back(osnd, orcv, s4, r4, slot, half)
 
-    def a1_take(k):
-        yp = y_peer(k)[0]
-        arrived(wa.at[core, z, yp], ra1.at[yp])
-
-    def b1_take(k):
-        zp = z_peer(k)[0]
-        arrived(wb.at[core, y, zp], rb1.at[zp])
-
-    each(NY, 1, a1_take)
-    push_each(NZ, a2_args)
-    each(NZ, 1, b1_take)
-    push_each(NY, b2_args)
     remote(*ca_args(z)).start()
-    remote(*cb_args(y)).start()
+    slab_store(core, z).start()
 
     for h in range(HEADS):
         cols = slice(h * DH, (h + 1) * DH)
@@ -735,54 +706,52 @@
         zp = z_peer(k)[0]
         arrived(wa.at[core, zp], ra2.at[zp])
         remote(*ca_args(zp)).start()
-        yp = y_peer(k)[0]
-        arrived(wb.at[core, yp], rb2.at[yp])
-        remote(*cb_args(yp)).start()
-
-    each(NY, 1, last_take)
-    store(wa.at[core], wa_out.at[core])
-    store(wb.at[core], wb_out.at[core])
+        slab_store(core, zp).start()
+
+    each(NZ, 1, last_take)
 
     def from_mate(at):
         arrived(wa.at[1 - core, at], rca.at[at])
-        arrived(wb.at[1 - core, at], rcb.at[at])
+        slab_store(1 - core, at).start()
         remote(*ca_args(at)).wait_send()
-        remote(*cb_args(at)).wait_send()
 
     each(NZ, 0, from_mate)
 
-    store(wa.at[1 - core], wa_out.at[1 - core])
-    store(wb.at[1 - core], wb_out.at[1 - core])
+    def slab_stored(at):
+        slab_store(0, at).wait()
+        slab_store(1, at).wait()
+
+    drains.append(lambda: each(NZ, 0, slab_stored))
 
     for drain in drains:
         drain()
 
 
 def writer(*refs):
-    ins, outs, held, sems = refs[:6], refs[6:11], refs[11:18], refs[18]
+    ins, outs, held, sems = refs[:5], refs[5:10], refs[10:16], refs[16]
+    wa_in, wa, gw = ins[4], held[4], held[5]
+    slabs = [
+        pltpu.make_async_copy(wa_in.at[:, zp], wa.at[:, zp], sems.at[zp]) for zp in range(NZ)
+    ]
     loads = [
-        pltpu.make_async_copy(src, dst, sems.at[at])
-        for at, (src, dst) in enumerate(zip(ins, held[:6], strict=True))
+        pltpu.make_async_copy(ins[at], held[at], sems.at[NZ + at]) for at in range(4)
     ]
-    for copy in loads[4:] + loads[:4]:
+    for copy in slabs + loads:
         copy.start()
-    wa, wb, gw = held[4:]
-    for copy in loads[4:]:
-        copy.wait()
     copies = []
     for zp in range(NZ):
+        slabs[zp].wait()
         for c in range(2):
             for at in range(NY):
                 first = zp * FEAT + at // 4 * (FEAT // 2)
                 cols = slice(c * HALF + at % 4 * BLK, c * HALF + at % 4 * BLK + BLK)
-                gw[first : first + 16, cols] = wa[c, zp, at].astype(F32)
-                gw[first + 16 : first + 32, cols] = wb[c, at, zp].astype(F32)
+                gw[first : first + FEAT // 2, cols] = wa[c, zp, at].astype(F32)
         rows = pl.ds(zp * FEAT, FEAT)
-        copies.append(pltpu.make_async_copy(gw.at[rows], outs[4].at[rows], sems.at[6 + zp]))
+        copies.append(pltpu.make_async_copy(gw.at[rows], outs[4].at[rows], sems.at[12 + zp]))
         copies[-1].start()
     for at in range(4):
         loads[at].wait()
-        copies.append(pltpu.make_async_copy(held[at], outs[at], sems.at[14 + at]))
+        copies.append(pltpu.make_async_copy(held[at], outs[at], sems.at[20 + at]))
         copies[-1].start()
     for copy in copies:
         copy.wait()
@@ -796,13 +765,13 @@
     grad_scale = 1.0 / math.sqrt(lax.axis_size("dp") * lax.axis_size("ctx") * rows)
     held = scratch()
     out_rows = jax.ShapeDtypeStruct((rows, features), BF)
-    slabs = jax.ShapeDtypeStruct((2, 8, 8, FEAT // 4, BLK), BF)
+    slabs = jax.ShapeDtypeStruct((2, NZ, NY, FEAT // 2, BLK), BF)
     anywhere = pl.BlockSpec(memory_space=pl.ANY)
     parts = pl.pallas_call(
         functools.partial(kernel, grad_scale),
-        out_shape=[out_rows] * 4 + [slabs] * 2,
+        out_shape=[out_rows] * 4 + [slabs],
         in_specs=[anywhere] * 8,
-        out_specs=[anywhere] * 6,
+        out_specs=[anywhere] * 5,
         scratch_shapes=list(held.values()),
         compiler_params=pltpu.CompilerParams(
             collective_id=0, has_side_effects=True, vmem_limit_bytes=VLIM * 1024 * 1024
@@ -820,13 +789,13 @@
     return pl.pallas_call(
         writer,
         out_shape=[out_rows] * 4 + [jax.ShapeDtypeStruct((features, width), F32)],
-        in_specs=[anywhere] * 6,
+        in_specs=[anywhere] * 5,
         out_specs=[anywhere] * 5,
         scratch_shapes=[
             *[pltpu.VMEM(out_rows.shape, BF)] * 4,
-            *[pltpu.VMEM(slabs.shape, BF)] * 2,
+            pltpu.VMEM(slabs.shape, BF),
             pltpu.VMEM((features, width), F32),
-            pltpu.SemaphoreType.DMA((18,)),
+            pltpu.SemaphoreType.DMA((24,)),
         ],
         compiler_params=pltpu.CompilerParams(vmem_limit_bytes=VLIM * 1024 * 1024),
     )(*parts)

time: 91.9 us -> 91.3 us (level)
  no operation moved by 1% of the time
where the time goes in v4:
time: 91.3 us; the launch traced here: 90.9 us
  Pallas kernels  90.3 us (99%)
    pallas_call x1, Pallas kernels, on_device(): pl.pallas_call(functools.partial(kernel, grad_scale), out_shape=[out_rows...  87.7 us
    pallas_call x1, Pallas kernels, on_device(): pl.pallas_call(writer, out_shape=[out_rows] * 4 + [jax.ShapeDtypeStruct((...  2.61 us

profile of v4, /device:TPU:1, one launch (start us, length us, event | category | flops | bytes accessed | tf_op | source)
XLA Modules:
  0.0 90.9 jit_solution(12967190499809923897)
XLA Ops:
  0.6 87.7 %shard_map.119 = (bf16[128,512]{1,0:T(8,128)(2,1)}, bf16[128,512]{1,0:T(8,128)(2,1)}, bf16[128,512]{1,0:T(8,128)(2,1)}, bf16[128,512]{1,0:T(8,128)(2,1)}, bf16[2,8,8,32,128]{4,3,2,1,0:T(8,128)(2,1)}) custom-call(bf16[128,512]{1,0:T(8,128)(2,1)} %refs_0_.1, bf16[128,512]{1,0:T(8,128)(2,1)} %refs_1_.1, bf16[128,512]{1,0:T(8,128)(2,1)} %refs_2_.1, ...), custom_call_target="tpu_custom_call" | custom-call | tf_op jit(solution)/shard_map/pallas_call | solution.py:770
  88.3 2.6 %shard_map.120 = (bf16[128,512]{1,0:T(8,128)(2,1)}, bf16[128,512]{1,0:T(8,128)(2,1)}, bf16[128,512]{1,0:T(8,128)(2,1)}, bf16[128,512]{1,0:T(8,128)(2,1)}, f32[512,1024]{1,0:T(8,128)}) custom-call(bf16[128,512]{1,0:T(8,128)(2,1)} %get-tuple-element.10.refs_0_, bf16[128,512]{1,0:T(8,128)(2,1)} %get-tuple-element.11.refs_1_, ...), custom_call_target="tpu_custom_call" | custom-call | tf_op jit(solution)/shard_map/pallas_call | solution.py:789

commit v5 on v4

--- a/solution.py
+++ b/solution.py
@@ -405,8 +405,6 @@
 
     hand_direct(0)
     hand_direct(1)
-    ring_up(ring_take(NZ - 1))
-    ring_down(ring_take(1))
     hand_direct(2)
     hand_direct(3)
     for h in range(HEADS):
@@ -418,6 +416,8 @@
             base + handler_core,
             handler_x * NY + core * HEADS + h,
         )
+    ring_up(ring_take(NZ - 1))
+    ring_down(ring_take(1))
     for at in range(4):
         hand_crossed(at)
     ring_up(ring_take(NZ - 2))

time: 91.3 us -> 92.5 us (1.013)
  Pallas kernels: 90.3 us -> 91.7 us
    pallas_call x1, Pallas kernels: 87.7 us -> 89.1 us  [on_device(): pl.pallas_call(functools.partial(kernel, grad_scale), out_shape=[out_rows...]
where the time goes in v5:
time: 92.5 us; the launch traced here: 92.3 us
  Pallas kernels  91.7 us (99%)
    pallas_call x1, Pallas kernels, on_device(): pl.pallas_call(functools.partial(kernel, grad_scale), out_shape=[out_rows...  89.1 us
    pallas_call x1, Pallas kernels, on_device(): pl.pallas_call(writer, out_shape=[out_rows] * 4 + [jax.ShapeDtypeStruct((...  2.61 us

profile of v5, /device:TPU:1, one launch (start us, length us, event | category | flops | bytes accessed | tf_op | source)
XLA Modules:
  0.0 92.3 jit_solution(9071864243536122667)
XLA Ops:
  0.6 89.1 %shard_map.119 = (bf16[128,512]{1,0:T(8,128)(2,1)}, bf16[128,512]{1,0:T(8,128)(2,1)}, bf16[128,512]{1,0:T(8,128)(2,1)}, bf16[128,512]{1,0:T(8,128)(2,1)}, bf16[2,8,8,32,128]{4,3,2,1,0:T(8,128)(2,1)}) custom-call(bf16[128,512]{1,0:T(8,128)(2,1)} %refs_0_.1, bf16[128,512]{1,0:T(8,128)(2,1)} %refs_1_.1, bf16[128,512]{1,0:T(8,128)(2,1)} %refs_2_.1, ...), custom_call_target="tpu_custom_call" | custom-call | tf_op jit(solution)/shard_map/pallas_call | solution.py:770
  89.7 2.6 %shard_map.120 = (bf16[128,512]{1,0:T(8,128)(2,1)}, bf16[128,512]{1,0:T(8,128)(2,1)}, bf16[128,512]{1,0:T(8,128)(2,1)}, bf16[128,512]{1,0:T(8,128)(2,1)}, f32[512,1024]{1,0:T(8,128)}) custom-call(bf16[128,512]{1,0:T(8,128)(2,1)} %get-tuple-element.10.refs_0_, bf16[128,512]{1,0:T(8,128)(2,1)} %get-tuple-element.11.refs_1_, ...), custom_call_target="tpu_custom_call" | custom-call | tf_op jit(solution)/shard_map/pallas_call | solution.py:789
